TPU v7x, 32 devices: a whole 2x2x4 slice. The times are simulated.
32 devices in a mesh: expert: 8 (over z, x), dp: 4 (over y, core).
Axes of the slice: x: 2, y: 2, z: 4, core: 2. Of those that a mesh axis runs over, the one named last changes fastest.
Arguments:
- tokens: bfloat16 [4096, 2048], P(('expert', 'dp')), may hold values from -6 to 6
- out_grad: bfloat16 [4096, 2048], P(('expert', 'dp')), may hold values from -6 to 6
- route_weights: bfloat16 [4096, 8], P(('expert', 'dp')), may hold values from 0.05 to 2.5, as said below
- expert_ids: int32 [4096, 8], P(('expert', 'dp')), may hold values from 0 to 15, all different within a row; in each aligned block of 128 rows (0 to 127, 128 to 255, ...) at most 96 rows name the same one
- gate_weight: bfloat16 [16, 2048, 384], P('expert'), may hold values from -0.125 to 0.125
- up_weight: bfloat16 [16, 2048, 384], P('expert'), may hold values from -0.125 to 0.125
- down_weight: bfloat16 [16, 384, 2048], P('expert'), may hold values from -0.3125 to 0.3125
Outputs:
- grad_input: bfloat16 [4096, 2048], P(('expert', 'dp'))
- grad_gate: bfloat16 [16, 2048, 384], P('expert', 'dp')
- grad_up: bfloat16 [16, 2048, 384], P('expert', 'dp')
- grad_down: bfloat16 [16, 384, 2048], P('expert', 'dp')
- expert_load: float32 [16], replicated
Inputs may be any that keep to these rules, and one draw needn't show every extreme that they name: `expert_ids`: each row names 8 different experts. Within each aligned block of 128 rows (the rows of one device) no expert is named by more than 96 rows, a bound that some block reaches. `route_weights`: positive router weights.
All inputs are finite; a program needn't handle non-finite values.
Results may differ from a plain program's by a relative error of at most 0.009.
Values may be sent and summed in bfloat16 or wider, within the bound.
No kernel may reach another device: no remote copies, remote signals or barrier semaphores. Data moves between devices by JAX's collectives and lax.ppermute only.
A program may use at most 192 MiB of HBM per device.

v0:
```python
import jax
import jax.numpy as jnp
from jax import lax
from jax.sharding import PartitionSpec as P

BF = jnp.bfloat16
F32 = jnp.float32
LANES = 128


def dot(a, b, ca, cb):
    return lax.dot_general(a, b, (((ca,), (cb,)), ((), ())), preferred_element_type=F32)


def tie(*values):
    return lax.optimization_barrier(values)


def shards(tokens, out_grad, route_weights, expert_ids, gate_weight, up_weight, down_weight):
    local_experts, width, hidden = gate_weight.shape
    devices = lax.axis_size("expert")
    groups = lax.axis_size("dp")
    num_experts = local_experts * devices
    rows, top_count = expert_ids.shape
    outer = devices // 2
    inner_width = local_experts * hidden
    me = lax.axis_index("expert")
    my_group = lax.axis_index("dp")

    def ring(value, step):
        pairs = [(2 * z + x, 2 * ((z + step) % outer) + x) for z in range(outer) for x in range(2)]
        return lax.ppermute(value, "expert", pairs)

    def cross(value):
        return lax.ppermute(value, "expert", [(i, i ^ 1) for i in range(devices)])

    def swap(value, bit):
        return lax.ppermute(value, "dp", [(i, i ^ bit) for i in range(groups)])

    lanes = jnp.arange(LANES, dtype=jnp.int32)
    dense = jnp.sum(
        jnp.where(
            expert_ids[:, :, None] == lanes, route_weights.astype(F32)[:, :, None], 0.0
        ),
        axis=1,
    ).astype(BF)
    grads = jnp.concatenate([out_grad, dense], axis=1)

    gate_up = jnp.concatenate(
        [gate_weight[e] for e in range(local_experts)] + [up_weight[e] for e in range(local_experts)],
        axis=1,
    )
    down_matrix = down_weight.reshape(inner_width, width)

    def middle(linear, grad_rows):
        cotangent = grad_rows[:, :width]
        routes = grad_rows[:, width:].astype(F32)
        weight = jnp.concatenate(
            [
                jnp.broadcast_to(
                    jnp.sum(
                        jnp.where(lanes == me * local_experts + e, routes, 0.0), axis=1, keepdims=True
                    ),
                    (grad_rows.shape[0], hidden),
                )
                for e in range(local_experts)
            ],
            axis=1,
        )
        gate_linear = linear[:, :inner_width]
        up_linear = linear[:, inner_width:]
        delta_hidden = weight * dot(cotangent, down_matrix, 1, 1)
        logistic = jax.nn.sigmoid(gate_linear)
        activated = gate_linear * logistic
        scaled_hidden = (weight * activated * up_linear).astype(BF)
        delta_gate = delta_hidden * up_linear * logistic * (1.0 + gate_linear * (1.0 - logistic))
        delta_up = delta_hidden * activated
        delta = jnp.concatenate([delta_gate.astype(BF), delta_up.astype(BF)], axis=1)
        return delta, scaled_hidden

    def partial_input(delta):
        return dot(delta, gate_up, 1, 1).astype(BF)

    near = my_group
    chunk_order = [near ^ 3, near ^ 2, near ^ 1, near]
    part = width // groups

    def stacked(blocks, axis=0):
        return jnp.concatenate(blocks, axis=axis) if len(blocks) > 1 else blocks[0]

    def by_chunk(blocks):
        return [
            stacked([lax.dynamic_slice(b, (0, c * part), (b.shape[0], part)) for b in blocks]) for c in chunk_order
        ]

    def cotangents(blocks):
        return stacked([g[:, :width] for g in blocks])

    def add(a, b):
        return (a.astype(F32) + b.astype(F32)).astype(BF)

    flying_a = (ring(tokens, 1), cross(tokens))
    flying_b = (ring(grads, 1), cross(grads))
    gate_up = tie(gate_up, grads)[0]
    token_blocks, grad_blocks, deltas, hiddens, own, other = [], [], [], [], [], []
    first_grad_cross = None
    for step in range(1, outer):
        got = tie(*flying_a, *((deltas[-1], hiddens[-1], own[-1], other[-1], first_grad_cross) if own else ()))
        if own:
            deltas[-1], hiddens[-1], own[-1], other[-1], first_grad_cross = got[2:]
        if step == outer - 1:
            flying_a = (cross(got[0]),)
            flying_back = (ring(first_grad_cross, outer - 1),)
        else:
            flying_a = (ring(got[0], 1), cross(got[0]))
        new_tokens = ((tokens,) if step == 1 else ()) + tuple(got[:2])
        token_blocks.append(new_tokens)
        linear = dot(stacked(new_tokens), gate_up, 1, 0)
        got = tie(*flying_b, linear)
        if step == 1:
            first_grad_cross = got[1]
        flying_b = flying_back if step == outer - 1 else (ring(got[0], 1), cross(got[0]))
        new_grads = ((grads,) if step == 1 else ()) + tuple(got[:2])
        grad_blocks.append(new_grads)
        delta, scaled_hidden = middle(got[2], stacked(new_grads))
        deltas.append(delta)
        hiddens.append(scaled_hidden)
        partial = partial_input(delta)
        if step == 1:
            own.append(partial[:rows])
        own.append(partial[-2 * rows : -rows])
        other.append(partial[-rows:])

    early = [t for blocks in token_blocks[:-1] for t in blocks]
    early_delta = stacked(deltas[:-1])
    early_gate_up = [dot(c, early_delta, 0, 0).astype(BF) for c in by_chunk(early)]
    early_down = dot(stacked(hiddens[:-1]), cotangents([g for b in grad_blocks[:-1] for g in b]), 0, 0).astype(BF)
    late_columns = by_chunk(token_blocks[-1])

    last_tokens, *got = tie(*flying_a, *own, *other)
    own, other = got[:outer], got[outer:]
    middle_step = outer // 2
    order = list(range(middle_step, 0, -1)) + list(range(middle_step + 1, outer - 1))
    crossed = {s: cross(other[s]) for s in order}
    late_columns = [stacked([a, b]) for a, b in zip(late_columns, by_chunk([last_tokens]))]
    linear = dot(last_tokens, gate_up, 1, 0)
    got = tie(*flying_b, linear, deltas[-1], hiddens[-1], early_down, *early_gate_up, *late_columns)
    last_grads, linear, deltas[-1], hiddens[-1], early_down = got[:5]
    early_gate_up, late_columns = got[5 : 5 + groups], got[5 + groups :]
    grad_blocks.append((last_grads,))
    load = sum(jnp.sum(g[:, width:].astype(F32), axis=0, keepdims=True) for b in grad_blocks for g in b)
    flying_load = swap(load, 1)
    delta, scaled_hidden = middle(linear, last_grads)
    late_delta = stacked([deltas[-1], delta])
    late_hidden = stacked([hiddens[-1], scaled_hidden])
    late_grads = cotangents([g for b in grad_blocks[-2:] for g in b])

    def whole_chunk(index, late_delta, received=None):
        value = dot(late_columns[index], late_delta, 0, 0) + early_gate_up[index].astype(F32)
        return (value if received is None else value + received.astype(F32)).astype(BF)

    def chunk(index, late_delta, kind, received=None):
        columns = slice(kind * inner_width, (kind + 1) * inner_width)
        value = dot(late_columns[index], late_delta[:, columns], 0, 0) + early_gate_up[index][:, columns].astype(F32)
        return (value if received is None else value + received.astype(F32)).astype(BF)

    def joined(up_part, down_part):
        size = part // 2
        down_part = down_part.reshape(-1, width)
        parts = [v[:, i : i + size] for v in (up_part, down_part) for i in range(0, v.shape[1], size)]
        return jnp.concatenate(parts, axis=0)

    def split(message):
        size = part // 2
        count = inner_width // size
        wide = jnp.concatenate([message[i * part : (i + 1) * part] for i in range(count)], axis=1)
        rest = message[count * part :]
        tall = local_experts * hidden // groups
        narrow = jnp.concatenate([rest[i * tall : (i + 1) * tall] for i in range(width // size)], axis=1)
        return wide, narrow.reshape(local_experts, hidden // groups, width)

    far_gate = chunk(0, late_delta, 0)
    flying_gate = swap(far_gate, 1)
    far_gate, late_delta = tie(far_gate, late_delta)
    far_up = chunk(0, late_delta, 1)
    flying_up = swap(far_up, 1)
    far_up, late_delta, flying_gate, flying_load = tie(far_up, late_delta, flying_gate, flying_load)
    load = load + flying_load
    flying_load = swap(load, 2)
    gate_sum = chunk(1, late_delta, 0, flying_gate)
    flying_gate = swap(gate_sum, 2)
    gate_sum, late_hidden, late_grads, late_delta, value = tie(
        gate_sum, late_hidden, late_grads, late_delta, crossed[middle_step]
    )
    minus = ring(add(own[middle_step], value), outer - 1)
    all_down = (dot(late_hidden, late_grads, 0, 0) + early_down.astype(F32)).astype(BF)
    all_down = all_down.reshape(local_experts, groups, hidden // groups, width)
    down = [lax.dynamic_index_in_dim(all_down, c, 1, keepdims=False) for c in chunk_order]
    flying_down = swap(down[0], 1)
    flying_up, late_delta, delta, *down = tie(flying_up, late_delta, delta, *down)
    up_sum = chunk(1, late_delta, 1, flying_up)
    up_sum, flying_down, delta, late_delta = tie(up_sum, flying_down, delta, late_delta)
    message = joined(up_sum, add(down[1], flying_down))
    flying_far = swap(message, 2)
    message, delta, late_delta, near_down, first_other = tie(message, delta, late_delta, down[2], other[0])
    last_partial = partial_input(delta)
    crossed[outer - 1] = cross(last_partial)
    near_sum = swap(whole_chunk(2, late_delta), 1)
    near_down = swap(near_down, 1)
    crossed[0] = cross(first_other)
    near_sum, near_down, late_delta = tie(near_sum, near_down, late_delta)
    near_sum = whole_chunk(3, late_delta, near_sum)
    near_gate, near_up = near_sum[:, :inner_width], near_sum[:, inner_width:]
    near_down = add(down[3], near_down)
    plus = None
    for s in range(middle_step - 1, 0, -1):
        minus, crossed[s], near_gate, near_up, near_down = tie(minus, crossed[s], near_gate, near_up, near_down)
        minus = ring((own[s].astype(F32) + crossed[s].astype(F32) + minus.astype(F32)).astype(BF), outer - 1)
    for s in range(middle_step + 1, outer):
        if plus is None:
            crossed[s], near_gate = tie(crossed[s], near_gate)
            plus = own[s].astype(F32) + crossed[s].astype(F32)
        else:
            crossed[s], plus, near_gate = tie(crossed[s], plus, near_gate)
            plus = own[s].astype(F32) + crossed[s].astype(F32) + plus.astype(F32)
        plus = ring(plus.astype(BF), 1)

    factor = 1.0 / groups

    def outputs(near, far):
        halves = []
        for e in range(local_experts):
            at = slice(e * hidden, (e + 1) * hidden)
            halves.append(((near[:, at].astype(F32) + far[:, at].astype(F32)) * factor).astype(BF))
        return jnp.stack(halves)

    flying_gate, near_gate = tie(flying_gate, near_gate)
    out_gate = outputs(near_gate, flying_gate)
    minus, plus, crossed[0], out_gate = tie(minus, plus, crossed[0], out_gate)
    grad_input = (
        own[0].astype(F32) + crossed[0].astype(F32) + minus.astype(F32) + plus.astype(F32)
    ).astype(BF)
    flying_far, flying_load, near_up, near_down, grad_input = tie(
        flying_far, flying_load, near_up, near_down, grad_input
    )
    load = load + flying_load
    expert_load = load[0, :num_experts] * (num_experts / (rows * devices * groups * top_count))
    far_up, far_down = split(flying_far)
    out_up = outputs(near_up, far_up)
    out_down = ((near_down.astype(F32) + far_down.astype(F32)) * factor).astype(BF)
    return (grad_input, out_gate, out_up, out_down, expert_load)


def solution(mesh):
    return jax.shard_map(
        shards,
        mesh=mesh,
        in_specs=(
            P(("expert", "dp"), None),
            P(("expert", "dp"), None),
            P(("expert", "dp"), None),
            P(("expert", "dp"), None),
            P("expert", None, None),
            P("expert", None, None),
            P("expert", None, None),
        ),
        out_specs=(
            P(("expert", "dp"), None),
            P("expert", "dp", None),
            P("expert", "dp", None),
            P("expert", "dp", None),
            P(),
        ),
        check_vma=False,
    )
```

profile of v0, /device:TPU:0, one launch (start us, length us, event | category | flops | bytes accessed | tf_op | source)
XLA Modules:
  0.0 162.9 jit_solution(17500974805697239395)
XLA Ops:
  0.6 3.0 %collective-permute-start.1 = (bf16[128,2048]{1,0:T(8,128)(2,1)}, bf16[128,2048]{1,0:T(8,128)(2,1)}, u32[]{:S(2)}, u32[]{:S(2)}) collective-permute-start(bf16[128,2048]{1,0:T(8,128)(2,1)} %param.7), channel_id=1, source_target_pairs={{0,4},{4,0},{8,12},{12,8},{16,20},{20,16},{24,28},{28,24},{1,5},{5... | collective-permute-start | bytes 1572872 | tf_op jit(solution)/shard_map/ppermute | solution.py:35
  3.7 1.6 collective-permute-start
  7.2 1.9 %pad_maximum_fusion.19 = bf16[128,2176]{1,0:T(8,128)(2,1)} fusion(bf16[128,128]{1,0:T(8,128)(2,1)S(1)} %select_reduce_fusion, bf16[128,2048]{1,0:T(8,128)(2,1)} %param.8), kind=kLoop, calls=%fused_computation.107 | loop fusion | flops 1114112 | bytes 1114112 | tf_op jit(solution)/shard_map/concatenate | solution.py:47
  9.6 1.6 collective-permute-start.4
  11.2 3.5 %slice_bitcast_fusion.1 = (bf16[2048,384]{1,0:T(8,128)(2,1)S(1)}, bf16[2048,384]{1,0:T(8,128)(2,1)S(1)}, bf16[2048,384]{1,0:T(8,128)(2,1)S(1)}, bf16[2048,384]{1,0:T(8,128)(2,1)S(1)}) fusion(bf16[2,2048,384]{2,1,0:T(8,128)(2,1)} %param.12, bf16[2,2048,384]{2,1,0:T(8,128)(2,1)} %param.11), kind=kLoop, calls=%fused_computation.38 | loop fusion | bytes 12582912 | tf_op jit(solution)/shard_map/squeeze | solution.py:50
  14.6 3.1 %pad_maximum_fusion = bf16[2048,1536]{1,0:T(8,128)(2,1)} fusion(bf16[2048,384]{1,0:T(8,128)(2,1)S(1)} %get-tuple-element.203, bf16[2048,384]{1,0:T(8,128)(2,1)S(1)} %get-tuple-element.202, bf16[2048,384]{1,0:T(8,128)(2,1)S(1)} %get-tuple-element.262, bf16[2048,384]{1,0:T(8,128)(2,1)S(1)} %get-tuple-element.263), kind=kLoop, calls=%fused_computation | loop fusion | flops 25165824 | bytes 12582912 | tf_op jit(solution)/shard_map/concatenate | solution.py:49
  17.8 1.1 dynamic-slice_dynamic-update-slice_fusion.4
  19.0 1.1 constant_dynamic-update-slice_fusion.4
  20.6 1.1 collective-permute-start.3
  21.7 1.6 collective-permute-start.2
  23.3 1.1 dynamic-slice_dynamic-update-slice_fusion.3
  24.4 1.1 dynamic-slice_dynamic-update-slice_fusion.2
  25.6 5.0 %fusion.5 = f32[384,1536]{1,0:T(8,128)S(1)} fusion(bf16[2048,1536]{1,0:T(8,128)(2,1)} %pad_maximum_fusion, bf16[128,2048]{1,0:T(8,128)(2,1)} %collective-permute-done.1, bf16[128,2048]{1,0:T(8,128)(2,1)} %collective-permute-done, bf16[128,2048]{1,0:T(8,128)(2,1)S(1)} %copy-done.5), kind=kOutput, calls=%fused_computation.21 | convolution fusion | flops 2420637696 | bytes 10223616 | tf_op jit(solution)/shard_map/dot_general | solution.py:12
  30.6 1.9 %collective-permute-done.4 = bf16[128,2176]{1,0:T(8,128)(2,1)} collective-permute-done((bf16[128,2176]{1,0:T(8,128)(2,1)}, bf16[128,2176]{1,0:T(8,128)(2,1)}, u32[]{:S(2)}, u32[]{:S(2)}) %collective-permute-start.4) | collective-permute-done | bytes 557088 | tf_op jit(solution)/shard_map/ppermute | solution.py:32
  34.9 3.3 %multiply_convert_fusion.1 = (bf16[384,768]{1,0:T(8,128)(2,1)S(1)}, bf16[384,768]{1,0:T(8,128)(2,1)S(1)}, bf16[384,768]{1,0:T(8,128)(2,1)S(1)}) fusion(f32[384,1536]{1,0:T(8,128)S(1)} %fusion.5, f32[384,384]{1,0:T(8,128)S(1)} %broadcast_in_dim.117, f32[384,384]{1,0:T(8,128)S(1)} %broadcast_in_dim.115, bf16[768,2048]{1,0:T(8,128)(2,1)S(1)} %bitcast.66, ...), kind=kOutput, calls=%fused_computation.52 | convolution fusion | flops 1219559424 | bytes 10125312 | tf_op jit(solution)/shard_map/dot_general | solution.py:12
  38.3 2.6 %convolution_convert_fusion.5 = bf16[384,2048]{1,0:T(8,128)(2,1)S(1)} fusion(bf16[2048,1536]{1,0:T(8,128)(2,1)S(1)} %bitcast.71, bf16[384,768]{1,0:T(8,128)(2,1)S(1)} %get-tuple-element.195, bf16[384,768]{1,0:T(8,128)(2,1)S(1)} %get-tuple-element.194), kind=kOutput, calls=%fused_computation.12 | convolution fusion | flops 2419064832 | bytes 9043968 | tf_op jit(solution)/shard_map/dot_general | solution.py:12
  40.9 1.1 slice_dynamic-update-slice_fusion.3
  42.0 1.1 slice_dynamic-update-slice_fusion.2
  44.1 1.8 %collective-permute-start.7 = (bf16[128,2048]{1,0:T(8,128)(2,1)S(1)}, bf16[128,2048]{1,0:T(8,128)(2,1)S(1)}, u32[]{:S(2)}, u32[]{:S(2)}) collective-permute-start(bf16[128,2048]{1,0:T(8,128)(2,1)S(1)} %collective-permute-done.2), channel_id=1, source_target_pairs={{0,4},{4,0},{8,12},{12,8},{16,20},{20,16},{24,28},{28,24},{1,5},{5... | collective-permute-start | bytes 1572872 | tf_op jit(solution)/shard_map/ppermute | solution.py:35
  45.8 1.4 collective-permute-start.6
  47.4 1.8 %fusion.20 = f32[256,1536]{1,0:T(8,128)S(1)} fusion(bf16[2048,1536]{1,0:T(8,128)(2,1)S(1)} %bitcast.71, bf16[128,2048]{1,0:T(8,128)(2,1)S(1)} %collective-permute-done.3, bf16[128,2048]{1,0:T(8,128)(2,1)S(1)} %collective-permute-done.2), kind=kOutput, calls=%fused_computation.57 | convolution fusion | flops 1612709888 | bytes 8912896 | tf_op jit(solution)/shard_map/dot_general | solution.py:12
  49.2 2.5 %collective-permute-done.9 = bf16[128,2176]{1,0:T(8,128)(2,1)S(1)} collective-permute-done((bf16[128,2176]{1,0:T(8,128)(2,1)}, bf16[128,2176]{1,0:T(8,128)(2,1)S(1)}, u32[]{:S(2)}, u32[]{:S(2)}) %collective-permute-start.9) | collective-permute-done | bytes 557088 | tf_op jit(solution)/shard_map/ppermute | solution.py:35
  51.7 3.9 %collective-permute-done.8 = bf16[128,2176]{1,0:T(8,128)(2,1)S(1)} collective-permute-done((bf16[128,2176]{1,0:T(8,128)(2,1)}, bf16[128,2176]{1,0:T(8,128)(2,1)S(1)}, u32[]{:S(2)}, u32[]{:S(2)}) %collective-permute-start.8) | collective-permute-done | bytes 557088 | tf_op jit(solution)/shard_map/ppermute | solution.py:32
  56.6 1.4 multiply_convert_fusion.9
  58.0 1.8 %convolution_convert_fusion.7 = bf16[256,2048]{1,0:T(8,128)(2,1)S(1)} fusion(bf16[2048,1536]{1,0:T(8,128)(2,1)S(1)} %bitcast.71, bf16[256,768]{1,0:T(8,128)(2,1)S(1)} %get-tuple-element.207, bf16[256,768]{1,0:T(8,128)(2,1)S(1)} %get-tuple-element.206), kind=kOutput, calls=%fused_computation.14 | convolution fusion | flops 1612709888 | bytes 8126464 | tf_op jit(solution)/shard_map/dot_general | solution.py:12
  60.0 3.0 %collective-permute-done.7 = bf16[128,2048]{1,0:T(8,128)(2,1)S(1)} collective-permute-done((bf16[128,2048]{1,0:T(8,128)(2,1)S(1)}, bf16[128,2048]{1,0:T(8,128)(2,1)S(1)}, u32[]{:S(2)}, u32[]{:S(2)}) %collective-permute-start.7) | collective-permute-done | bytes 524320 | tf_op jit(solution)/shard_map/ppermute | solution.py:35
  63.0 3.9 %collective-permute-done.6 = bf16[128,2048]{1,0:T(8,128)(2,1)S(1)} collective-permute-done((bf16[128,2048]{1,0:T(8,128)(2,1)S(1)}, bf16[128,2048]{1,0:T(8,128)(2,1)S(1)}, u32[]{:S(2)}, u32[]{:S(2)}) %collective-permute-start.6) | collective-permute-done | bytes 524320 | tf_op jit(solution)/shard_map/ppermute | solution.py:32
  67.3 1.4 convolution_convert_fusion.1
  68.7 1.4 convolution_convert_fusion.2
  70.2 1.4 convolution_convert_fusion.3
  71.6 1.4 convolution_convert_fusion.4
  73.0 4.0 %convolution_convert_fusion = bf16[768,2048]{1,0:T(8,128)(2,1)} fusion(bf16[640,2048]{1,0:T(8,128)(2,1)S(1)} %slice_dynamic-update-slice_fusion, bf16[256,768]{1,0:T(8,128)(2,1)S(1)} %get-tuple-element.119, bf16[384,768]{1,0:T(8,128)(2,1)S(1)} %get-tuple-element.118), kind=kOutput, calls=%fused_computation.2 | convolution fusion | flops 2016804864 | bytes 6750208 | tf_op jit(solution)/shard_map/dot_general | solution.py:12
  77.1 2.3 %collective-permute-start.10 = (bf16[128,2176]{1,0:T(8,128)(2,1)}, bf16[128,2176]{1,0:T(8,128)(2,1)S(1)}, u32[]{:S(2)}, u32[]{:S(2)}) collective-permute-start(bf16[128,2176]{1,0:T(8,128)(2,1)} %collective-permute-done.5), channel_id=1, source_target_pairs={{0,24},{4,28},{8,0},{12,4},{16,8},{20,12},{24,16},{28,20},{1,25},{... | collective-permute-start | bytes 1671176 | tf_op jit(solution)/shard_map/ppermute | solution.py:32
  79.4 1.8 %fusion.24 = f32[256,1536]{1,0:T(8,128)S(1)} fusion(bf16[2048,1536]{1,0:T(8,128)(2,1)S(1)} %bitcast.71, bf16[128,2048]{1,0:T(8,128)(2,1)S(1)} %collective-permute-done.7, bf16[128,2048]{1,0:T(8,128)(2,1)S(1)} %collective-permute-done.6), kind=kOutput, calls=%fused_computation.61 | convolution fusion | flops 1612709888 | bytes 8912896 | tf_op jit(solution)/shard_map/dot_general | solution.py:12
  81.7 1.4 multiply_convert_fusion.7
  83.2 1.8 %convolution_convert_fusion.6 = bf16[256,2048]{1,0:T(8,128)(2,1)S(1)} fusion(bf16[2048,1536]{1,0:T(8,128)(2,1)S(1)} %bitcast.71, bf16[256,768]{1,0:T(8,128)(2,1)S(1)} %get-tuple-element.205, bf16[256,768]{1,0:T(8,128)(2,1)S(1)} %get-tuple-element.204), kind=kOutput, calls=%fused_computation.13 | convolution fusion | flops 1612709888 | bytes 8126464 | tf_op jit(solution)/shard_map/dot_general | solution.py:12
  85.3 1.8 %collective-permute-start.17 = (bf16[128,2048]{1,0:T(8,128)(2,1)S(1)}, bf16[128,2048]{1,0:T(8,128)(2,1)S(1)}, u32[]{:S(2)}, u32[]{:S(2)}) collective-permute-start(bf16[128,2048]{1,0:T(8,128)(2,1)S(1)} %get-tuple-element.133), channel_id=1, source_target_pairs={{0,4},{4,0},{8,12},{12,8},{16,20},{20,16},{24,28},{28,24},{1,5},{5... | collective-permute-start | bytes 1572872 | tf_op jit(solution)/shard_map/ppermute | solution.py:35
  87.3 1.0 fusion.72
  88.3 1.3 collective-permute-done.10
  90.0 1.3 multiply_convert_fusion.11
  95.2 3.3 %collective-permute-done.17 = bf16[128,2048]{1,0:T(8,128)(2,1)S(1)} collective-permute-done((bf16[128,2048]{1,0:T(8,128)(2,1)S(1)}, bf16[128,2048]{1,0:T(8,128)(2,1)S(1)}, u32[]{:S(2)}, u32[]{:S(2)}) %collective-permute-start.17) | collective-permute-done | bytes 524320 | tf_op jit(solution)/shard_map/ppermute | solution.py:35
  98.5 1.9 %add_convert_fusion = bf16[768,2048]{1,0:T(8,128)(2,1)S(1)} fusion(bf16[768,2048]{1,0:T(8,128)(2,1)S(1)} %copy-done.6, bf16[384,768]{1,0:T(8,128)(2,1)S(1)} %pad_maximum_fusion.18, bf16[384,2048]{1,0:T(8,128)(2,1)S(1)} %pad_maximum_fusion.7), kind=kOutput, calls=%fused_computation.1 | convolution fusion | flops 1212678144 | bytes 8454144 | tf_op jit(solution)/shard_map/dot_general | solution.py:12
  101.7 1.3 collective-permute-done.18
  103.6 1.3 fusion.1
  105.0 1.4 collective-permute-start.22
  106.5 1.5 collective-permute-start.29
  108.1 3.7 %collective-permute-start.21 = (bf16[128,2048]{1,0:T(8,128)(2,1)S(1)}, bf16[128,2048]{1,0:T(8,128)(2,1)S(1)}, u32[]{:S(2)}, u32[]{:S(2)}) collective-permute-start(bf16[128,2048]{1,0:T(8,128)(2,1)S(1)} %add_convert_fusion.10), channel_id=1, source_target_pairs={{0,24},{4,28},{8,0},{12,4},{16,8},{20,12},{24,16},{28,20},{1,25},{... | collective-permute-start | bytes 1572872 | tf_op jit(solution)/shard_map/ppermute | solution.py:32
  111.8 2.1 %convolution_convert_fusion.8 = bf16[128,2048]{1,0:T(8,128)(2,1)S(1)} fusion(bf16[128,1536]{1,0:T(8,128)(2,1)S(1)} %pad_maximum_fusion.27, bf16[2048,1536]{1,0:T(8,128)(2,1)S(1)} %bitcast.71), kind=kOutput, calls=%fused_computation.15 | convolution fusion | flops 805568512 | bytes 7208960 | tf_op jit(solution)/shard_map/dot_general | solution.py:12
  115.1 1.2 fusion.2
  116.6 3.2 %collective-permute-done.22 = bf16[128,2048]{1,0:T(8,128)(2,1)S(1)} collective-permute-done((bf16[128,2048]{1,0:T(8,128)(2,1)S(1)}, bf16[128,2048]{1,0:T(8,128)(2,1)S(1)}, u32[]{:S(2)}, u32[]{:S(2)}) %collective-permute-start.22) | collective-permute-done | bytes 524320 | tf_op jit(solution)/shard_map/ppermute | solution.py:35
  119.8 1.4 collective-permute-start.28
  121.2 2.4 %collective-permute-done.21 = bf16[128,2048]{1,0:T(8,128)(2,1)S(1)} collective-permute-done((bf16[128,2048]{1,0:T(8,128)(2,1)S(1)}, bf16[128,2048]{1,0:T(8,128)(2,1)S(1)}, u32[]{:S(2)}, u32[]{:S(2)}) %collective-permute-start.21) | collective-permute-done | bytes 524320 | tf_op jit(solution)/shard_map/ppermute | solution.py:32
  123.7 7.4 %collective-permute-done.26 = bf16[128,2048]{1,0:T(8,128)(2,1)S(1)} collective-permute-done((bf16[128,2048]{1,0:T(8,128)(2,1)S(1)}, bf16[128,2048]{1,0:T(8,128)(2,1)S(1)}, u32[]{:S(2)}, u32[]{:S(2)}) %collective-permute-start.26) | collective-permute-done | bytes 524320 | tf_op jit(solution)/shard_map/ppermute | solution.py:35
  131.2 1.6 collective-permute-start.27
  133.0 2.4 %collective-permute-start.25 = (bf16[128,2048]{1,0:T(8,128)(2,1)S(1)}, bf16[128,2048]{1,0:T(8,128)(2,1)S(1)}, u32[]{:S(2)}, u32[]{:S(2)}) collective-permute-start(bf16[128,2048]{1,0:T(8,128)(2,1)S(1)} %add_convert_fusion.9), channel_id=1, source_target_pairs={{0,24},{4,28},{8,0},{12,4},{16,8},{20,12},{24,16},{28,20},{1,25},{... | collective-permute-start | bytes 1572872 | tf_op jit(solution)/shard_map/ppermute | solution.py:32
  135.4 1.5 collective-permute-start.20
  137.1 1.0 pad_maximum_fusion.16
  138.0 3.7 %collective-permute-done.28 = bf16[128,2048]{1,0:T(8,128)(2,1)S(1)} collective-permute-done((bf16[128,2048]{1,0:T(8,128)(2,1)S(1)}, bf16[128,2048]{1,0:T(8,128)(2,1)S(1)}, u32[]{:S(2)}, u32[]{:S(2)}) %collective-permute-start.28) | collective-permute-done | bytes 524320 | tf_op jit(solution)/shard_map/ppermute | solution.py:35
  141.7 6.2 %collective-permute-done.27 = bf16[128,2048]{1,0:T(8,128)(2,1)S(1)} collective-permute-done((bf16[128,2048]{1,0:T(8,128)(2,1)S(1)}, bf16[128,2048]{1,0:T(8,128)(2,1)S(1)}, u32[]{:S(2)}, u32[]{:S(2)}) %collective-permute-start.27) | collective-permute-done | bytes 524320 | tf_op jit(solution)/shard_map/ppermute | solution.py:32
  147.9 8.9 %collective-permute-done.25 = bf16[128,2048]{1,0:T(8,128)(2,1)S(1)} collective-permute-done((bf16[128,2048]{1,0:T(8,128)(2,1)S(1)}, bf16[128,2048]{1,0:T(8,128)(2,1)S(1)}, u32[]{:S(2)}, u32[]{:S(2)}) %collective-permute-start.25) | collective-permute-done | bytes 524320 | tf_op jit(solution)/shard_map/ppermute | solution.py:32
  156.8 1.1 add_convert_fusion.7
  158.0 1.8 %collective-permute-done.20 = f32[1,128]{1,0:T(1,128)S(1)} collective-permute-done((f32[1,128]{1,0:T(1,128)S(1)}, f32[1,128]{1,0:T(1,128)S(1)}, u32[]{:S(2)}, u32[]{:S(2)}) %collective-permute-start.20) | collective-permute-done | bytes 544 | tf_op jit(solution)/shard_map/ppermute | solution.py:38
  160.7 1.0 pad_maximum_fusion.17
  161.7 1.2 fusion.12
  (143 shorter events, 18.3 us)
Async XLA Ops:
  0.6 33.9 %copy-start = (bf16[2,384,2048]{2,1,0:T(8,128)(2,1)S(1)}, bf16[2,384,2048]{2,1,0:T(8,128)(2,1)}, u32[]{:S(2)}) copy-start(bf16[2,384,2048]{2,1,0:T(8,128)(2,1)} %param.13) | copy-start | bytes 9437188
  0.6 19.5 %collective-permute-start.1 = (bf16[128,2048]{1,0:T(8,128)(2,1)}, bf16[128,2048]{1,0:T(8,128)(2,1)}, u32[]{:S(2)}, u32[]{:S(2)}) collective-permute-start(bf16[128,2048]{1,0:T(8,128)(2,1)} %param.7), channel_id=1, source_target_pairs={{0,4},{4,0},{8,12},{12,8},{16,20},{20,16},{24,28},{28,24},{1,5},{5... | collective-permute-start | bytes 1572872 | tf_op jit(solution)/shard_map/ppermute | solution.py:35
  3.7 17.0 %collective-permute-start = (bf16[128,2048]{1,0:T(8,128)(2,1)}, bf16[128,2048]{1,0:T(8,128)(2,1)}, u32[]{:S(2)}, u32[]{:S(2)}) collective-permute-start(bf16[128,2048]{1,0:T(8,128)(2,1)} %param.7), channel_id=1, source_target_pairs={{0,8},{4,12},{8,16},{12,20},{16,24},{20,28},{24,0},{28,4},{1,9},{5... | collective-permute-start | bytes 1572872 | tf_op jit(solution)/shard_map/ppermute | solution.py:32
  9.1 21.6 %collective-permute-start.5 = (bf16[128,2176]{1,0:T(8,128)(2,1)}, bf16[128,2176]{1,0:T(8,128)(2,1)}, u32[]{:S(2)}, u32[]{:S(2)}) collective-permute-start(bf16[128,2176]{1,0:T(8,128)(2,1)} %pad_maximum_fusion.19), channel_id=1, source_target_pairs={{0,4},{4,0},{8,12},{12,8},{16,20},{20,16},{24,28},{28,24},{1,5},{5... | collective-permute-start | bytes 1671176 | tf_op jit(solution)/shard_map/ppermute | solution.py:35
  9.6 23.0 %collective-permute-start.4 = (bf16[128,2176]{1,0:T(8,128)(2,1)}, bf16[128,2176]{1,0:T(8,128)(2,1)}, u32[]{:S(2)}, u32[]{:S(2)}) collective-permute-start(bf16[128,2176]{1,0:T(8,128)(2,1)} %pad_maximum_fusion.19), channel_id=1, source_target_pairs={{0,8},{4,12},{8,16},{12,20},{16,24},{20,28},{24,0},{28,4},{1,9},{5... | collective-permute-start | bytes 1671176 | tf_op jit(solution)/shard_map/ppermute | solution.py:32
  18.9 6.6 %copy-start.5 = (bf16[128,2048]{1,0:T(8,128)(2,1)S(1)}, bf16[128,2048]{1,0:T(8,128)(2,1)}, u32[]{:S(2)}) copy-start(bf16[128,2048]{1,0:T(8,128)(2,1)} %param.7) | copy-start | bytes 1572868
  20.6 23.4 %collective-permute-start.3 = (bf16[128,2048]{1,0:T(8,128)(2,1)}, bf16[128,2048]{1,0:T(8,128)(2,1)S(1)}, u32[]{:S(2)}, u32[]{:S(2)}) collective-permute-start(bf16[128,2048]{1,0:T(8,128)(2,1)} %collective-permute-done), channel_id=1, source_target_pairs={{0,4},{4,0},{8,12},{12,8},{16,20},{20,16},{24,28},{28,24},{1,5},{5... | collective-permute-start | bytes 1572872 | tf_op jit(solution)/shard_map/ppermute | solution.py:35
  21.7 22.4 %collective-permute-start.2 = (bf16[128,2048]{1,0:T(8,128)(2,1)}, bf16[128,2048]{1,0:T(8,128)(2,1)S(1)}, u32[]{:S(2)}, u32[]{:S(2)}) collective-permute-start(bf16[128,2048]{1,0:T(8,128)(2,1)} %collective-permute-done), channel_id=1, source_target_pairs={{0,8},{4,12},{8,16},{12,20},{16,24},{20,28},{24,0},{28,4},{1,9},{5... | collective-permute-start | bytes 1572872 | tf_op jit(solution)/shard_map/ppermute | solution.py:32
  25.5 8.1 %copy-start.1 = (bf16[128,2048]{1,0:T(8,128)(2,1)S(1)}, bf16[128,2048]{1,0:T(8,128)(2,1)}, u32[]{:S(2)}) copy-start(bf16[128,2048]{1,0:T(8,128)(2,1)} %param.8) | copy-start | bytes 1572868
  32.5 19.2 %collective-permute-start.9 = (bf16[128,2176]{1,0:T(8,128)(2,1)}, bf16[128,2176]{1,0:T(8,128)(2,1)S(1)}, u32[]{:S(2)}, u32[]{:S(2)}) collective-permute-start(bf16[128,2176]{1,0:T(8,128)(2,1)} %collective-permute-done.4), channel_id=1, source_target_pairs={{0,4},{4,0},{8,12},{12,8},{16,20},{20,16},{24,28},{28,24},{1,5},{5... | collective-permute-start | bytes 1671176 | tf_op jit(solution)/shard_map/ppermute | solution.py:35
  32.9 22.7 %collective-permute-start.8 = (bf16[128,2176]{1,0:T(8,128)(2,1)}, bf16[128,2176]{1,0:T(8,128)(2,1)S(1)}, u32[]{:S(2)}, u32[]{:S(2)}) collective-permute-start(bf16[128,2176]{1,0:T(8,128)(2,1)} %collective-permute-done.4), channel_id=1, source_target_pairs={{0,8},{4,12},{8,16},{12,20},{16,24},{20,28},{24,0},{28,4},{1,9},{5... | collective-permute-start | bytes 1671176 | tf_op jit(solution)/shard_map/ppermute | solution.py:32
  34.7 3.5 %slice-start = ((s8[6291456]{0:T(1024)(128)(4,1)}), s8[4194304]{0:T(1024)(128)(4,1)S(1)}, s32[]{:S(2)}) async-start(s8[6291456]{0:T(1024)(128)(4,1)} %bitcast.70), calls=%async_computation | async-start | bytes 8388608
  34.8 3.4 %slice-start.1 = ((s8[6291456]{0:T(1024)(128)(4,1)}), s8[2097152]{0:T(1024)(128)(4,1)S(1)}, s32[]{:S(2)}) async-start(s8[6291456]{0:T(1024)(128)(4,1)} %bitcast.70), calls=%async_computation.1 | async-start | bytes 4194304
  44.1 18.9 %collective-permute-start.7 = (bf16[128,2048]{1,0:T(8,128)(2,1)S(1)}, bf16[128,2048]{1,0:T(8,128)(2,1)S(1)}, u32[]{:S(2)}, u32[]{:S(2)}) collective-permute-start(bf16[128,2048]{1,0:T(8,128)(2,1)S(1)} %collective-permute-done.2), channel_id=1, source_target_pairs={{0,4},{4,0},{8,12},{12,8},{16,20},{20,16},{24,28},{28,24},{1,5},{5... | collective-permute-start | bytes 1572872 | tf_op jit(solution)/shard_map/ppermute | solution.py:35
  45.8 21.0 %collective-permute-start.6 = (bf16[128,2048]{1,0:T(8,128)(2,1)S(1)}, bf16[128,2048]{1,0:T(8,128)(2,1)S(1)}, u32[]{:S(2)}, u32[]{:S(2)}) collective-permute-start(bf16[128,2048]{1,0:T(8,128)(2,1)S(1)} %collective-permute-done.2), channel_id=1, source_target_pairs={{0,8},{4,12},{8,16},{12,20},{16,24},{20,28},{24,0},{28,4},{1,9},{5... | collective-permute-start | bytes 1572872 | tf_op jit(solution)/shard_map/ppermute | solution.py:32
  55.6 25.6 %collective-permute-start.13 = (bf16[128,2176]{1,0:T(8,128)(2,1)S(1)}, bf16[128,2176]{1,0:T(8,128)(2,1)S(1)}, u32[]{:S(2)}, u32[]{:S(2)}) collective-permute-start(bf16[128,2176]{1,0:T(8,128)(2,1)S(1)} %collective-permute-done.8), channel_id=1, source_target_pairs={{0,4},{4,0},{8,12},{12,8},{16,20},{20,16},{24,28},{28,24},{1,5},{5... | collective-permute-start | bytes 1671176 | tf_op jit(solution)/shard_map/ppermute | solution.py:35
  56.0 25.2 %collective-permute-start.12 = (bf16[128,2176]{1,0:T(8,128)(2,1)S(1)}, bf16[128,2176]{1,0:T(8,128)(2,1)S(1)}, u32[]{:S(2)}, u32[]{:S(2)}) collective-permute-start(bf16[128,2176]{1,0:T(8,128)(2,1)S(1)} %collective-permute-done.8), channel_id=1, source_target_pairs={{0,8},{4,12},{8,16},{12,20},{16,24},{20,28},{24,0},{28,4},{1,9},{5... | collective-permute-start | bytes 1671176 | tf_op jit(solution)/shard_map/ppermute | solution.py:32
  66.9 18.4 %collective-permute-start.11 = (bf16[128,2048]{1,0:T(8,128)(2,1)S(1)}, bf16[128,2048]{1,0:T(8,128)(2,1)S(1)}, u32[]{:S(2)}, u32[]{:S(2)}) collective-permute-start(bf16[128,2048]{1,0:T(8,128)(2,1)S(1)} %collective-permute-done.6), channel_id=1, source_target_pairs={{0,4},{4,0},{8,12},{12,8},{16,20},{20,16},{24,28},{28,24},{1,5},{5... | collective-permute-start | bytes 1572872 | tf_op jit(solution)/shard_map/ppermute | solution.py:35
  77.1 12.6 %collective-permute-start.10 = (bf16[128,2176]{1,0:T(8,128)(2,1)}, bf16[128,2176]{1,0:T(8,128)(2,1)S(1)}, u32[]{:S(2)}, u32[]{:S(2)}) collective-permute-start(bf16[128,2176]{1,0:T(8,128)(2,1)} %collective-permute-done.5), channel_id=1, source_target_pairs={{0,24},{4,28},{8,0},{12,4},{16,8},{20,12},{24,16},{28,20},{1,25},{... | collective-permute-start | bytes 1671176 | tf_op jit(solution)/shard_map/ppermute | solution.py:32
  81.2 3.8 %copy-start.2 = (bf16[128,2176]{1,0:T(8,128)(2,1)}, bf16[128,2176]{1,0:T(8,128)(2,1)S(1)}, u32[]{:S(2)}) copy-start(bf16[128,2176]{1,0:T(8,128)(2,1)S(1)} %collective-permute-done.13) | copy-start | bytes 1671172
  81.2 3.8 %copy-start.3 = (bf16[128,2176]{1,0:T(8,128)(2,1)}, bf16[128,2176]{1,0:T(8,128)(2,1)S(1)}, u32[]{:S(2)}) copy-start(bf16[128,2176]{1,0:T(8,128)(2,1)S(1)} %collective-permute-done.12) | copy-start | bytes 1671172
  85.3 13.2 %collective-permute-start.17 = (bf16[128,2048]{1,0:T(8,128)(2,1)S(1)}, bf16[128,2048]{1,0:T(8,128)(2,1)S(1)}, u32[]{:S(2)}, u32[]{:S(2)}) collective-permute-start(bf16[128,2048]{1,0:T(8,128)(2,1)S(1)} %get-tuple-element.133), channel_id=1, source_target_pairs={{0,4},{4,0},{8,12},{12,8},{16,20},{20,16},{24,28},{28,24},{1,5},{5... | collective-permute-start | bytes 1572872 | tf_op jit(solution)/shard_map/ppermute | solution.py:35
  89.6 2.4 %copy-start.4 = (bf16[128,2176]{1,0:T(8,128)(2,1)}, bf16[128,2176]{1,0:T(8,128)(2,1)S(1)}, u32[]{:S(2)}) copy-start(bf16[128,2176]{1,0:T(8,128)(2,1)S(1)} %collective-permute-done.10) | copy-start | bytes 1671172
  91.9 2.4 %collective-permute-start.15 = (bf16[512,768]{1,0:T(8,128)(2,1)S(1)}, bf16[512,768]{1,0:T(8,128)(2,1)S(1)}, u32[]{:S(2)}, u32[]{:S(2)}) collective-permute-start(bf16[512,768]{1,0:T(8,128)(2,1)S(1)} %add_convert_fusion.6), channel_id=1, source_target_pairs={{0,1},{1,0},{2,3},{3,2},{4,5},{5,4},{6,7},{7,6},{8,9},{9,8},{10,11... | collective-permute-start | bytes 2359304 | tf_op jit(solution)/shard_map/ppermute | solution.py:38
  92.1 1.3 slice-start.2
  92.1 1.3 slice-start.3
  92.1 1.3 slice-start.4
  92.1 2.2 %collective-permute-start.16 = (f32[1,128]{1,0:T(1,128)S(1)}, f32[1,128]{1,0:T(1,128)S(1)}, u32[]{:S(2)}, u32[]{:S(2)}) collective-permute-start(f32[1,128]{1,0:T(1,128)S(1)} %add_bitcast_fusion), channel_id=1, source_target_pairs={{0,1},{1,0},{2,3},{3,2},{4,5},{5,4},{6,7},{7,6},{8,9},{9,8},{10,11... | collective-permute-start | bytes 1544 | tf_op jit(solution)/shard_map/ppermute | solution.py:38
  93.2 7.6 %collective-permute-start.14 = (bf16[512,768]{1,0:T(8,128)(2,1)S(1)}, bf16[512,768]{1,0:T(8,128)(2,1)S(1)}, u32[]{:S(2)}, u32[]{:S(2)}) collective-permute-start(bf16[512,768]{1,0:T(8,128)(2,1)S(1)} %add_convert_fusion.5), channel_id=1, source_target_pairs={{0,1},{1,0},{2,3},{3,2},{4,5},{5,4},{6,7},{7,6},{8,9},{9,8},{10,11... | collective-permute-start | bytes 2359304 | tf_op jit(solution)/shard_map/ppermute | solution.py:38
  94.9 3.6 %copy-start.6 = (bf16[768,2048]{1,0:T(8,128)(2,1)S(1)}, bf16[768,2048]{1,0:T(8,128)(2,1)}, u32[]{:S(2)}) copy-start(bf16[768,2048]{1,0:T(8,128)(2,1)} %convolution_convert_fusion) | copy-start | bytes 9437188
  100.7 2.4 %collective-permute-start.18 = (bf16[2,96,2048]{2,1,0:T(8,128)(2,1)S(1)}, bf16[2,96,2048]{2,1,0:T(8,128)(2,1)S(1)}, u32[]{:S(2)}, u32[]{:S(2)}) collective-permute-start(bf16[2,96,2048]{2,1,0:T(8,128)(2,1)S(1)} %get-tuple-element.199), channel_id=1, source_target_pairs={{0,1},{1,0},{2,3},{3,2},{4,5},{5,4},{6,7},{7,6},{8,9},{9,8},{10,11... | collective-permute-start | bytes 2359304 | tf_op jit(solution)/shard_map/ppermute | solution.py:38
  104.8 9.7 %collective-permute-start.23 = (bf16[512,1536]{1,0:T(8,128)(2,1)S(1)}, bf16[512,1536]{1,0:T(8,128)(2,1)S(1)}, u32[]{:S(2)}, u32[]{:S(2)}) collective-permute-start(bf16[512,1536]{1,0:T(8,128)(2,1)S(1)} %fusion.1), channel_id=1, source_target_pairs={{0,1},{1,0},{2,3},{3,2},{4,5},{5,4},{6,7},{7,6},{8,9},{9,8},{10,11... | collective-permute-start | bytes 4718600 | tf_op jit(solution)/shard_map/ppermute | solution.py:38
  105.0 14.8 %collective-permute-start.22 = (bf16[128,2048]{1,0:T(8,128)(2,1)S(1)}, bf16[128,2048]{1,0:T(8,128)(2,1)S(1)}, u32[]{:S(2)}, u32[]{:S(2)}) collective-permute-start(bf16[128,2048]{1,0:T(8,128)(2,1)S(1)} %get-tuple-element.147), channel_id=1, source_target_pairs={{0,4},{4,0},{8,12},{12,8},{16,20},{20,16},{24,28},{28,24},{1,5},{5... | collective-permute-start | bytes 1572872 | tf_op jit(solution)/shard_map/ppermute | solution.py:35
  106.5 28.9 %collective-permute-start.29 = (bf16[512,768]{1,0:T(8,128)(2,1)S(1)}, bf16[512,768]{1,0:T(8,128)(2,1)S(1)}, u32[]{:S(2)}, u32[]{:S(2)}) collective-permute-start(bf16[512,768]{1,0:T(8,128)(2,1)S(1)} %add_convert_fusion.4), channel_id=1, source_target_pairs={{0,2},{1,3},{2,0},{3,1},{4,6},{5,7},{6,4},{7,5},{8,10},{9,11},{10,... | collective-permute-start | bytes 2359304 | tf_op jit(solution)/shard_map/ppermute | solution.py:38
  108.0 5.9 %collective-permute-start.24 = (bf16[2,96,2048]{2,1,0:T(8,128)(2,1)S(1)}, bf16[2,96,2048]{2,1,0:T(8,128)(2,1)S(1)}, u32[]{:S(2)}, u32[]{:S(2)}) collective-permute-start(bf16[2,96,2048]{2,1,0:T(8,128)(2,1)S(1)} %get-tuple-element.156), channel_id=1, source_target_pairs={{0,1},{1,0},{2,3},{3,2},{4,5},{5,4},{6,7},{7,6},{8,9},{9,8},{10,11... | collective-permute-start | bytes 2359304 | tf_op jit(solution)/shard_map/ppermute | solution.py:38
  108.1 15.5 %collective-permute-start.21 = (bf16[128,2048]{1,0:T(8,128)(2,1)S(1)}, bf16[128,2048]{1,0:T(8,128)(2,1)S(1)}, u32[]{:S(2)}, u32[]{:S(2)}) collective-permute-start(bf16[128,2048]{1,0:T(8,128)(2,1)S(1)} %add_convert_fusion.10), channel_id=1, source_target_pairs={{0,24},{4,28},{8,0},{12,4},{16,8},{20,12},{24,16},{28,20},{1,25},{... | collective-permute-start | bytes 1572872 | tf_op jit(solution)/shard_map/ppermute | solution.py:32
  114.0 45.8 %collective-permute-start.19 = (bf16[3072,256]{1,0:T(8,128)(2,1)S(1)}, bf16[3072,256]{1,0:T(8,128)(2,1)S(1)}, u32[]{:S(2)}, u32[]{:S(2)}) collective-permute-start(bf16[3072,256]{1,0:T(8,128)(2,1)S(1)} %constant_dynamic-update-slice_fusion.7), channel_id=1, source_target_pairs={{0,2},{1,3},{2,0},{3,1},{4,6},{5,7},{6,4},{7,5},{8,10},{9,11},{10,... | collective-permute-start | bytes 4718600 | tf_op jit(solution)/shard_map/ppermute | solution.py:38
  114.5 16.5 %collective-permute-start.26 = (bf16[128,2048]{1,0:T(8,128)(2,1)S(1)}, bf16[128,2048]{1,0:T(8,128)(2,1)S(1)}, u32[]{:S(2)}, u32[]{:S(2)}) collective-permute-start(bf16[128,2048]{1,0:T(8,128)(2,1)S(1)} %convolution_convert_fusion.8), channel_id=1, source_target_pairs={{0,4},{4,0},{8,12},{12,8},{16,20},{20,16},{24,28},{28,24},{1,5},{5... | collective-permute-start | bytes 1572872 | tf_op jit(solution)/shard_map/ppermute | solution.py:35
  119.8 21.9 %collective-permute-start.28 = (bf16[128,2048]{1,0:T(8,128)(2,1)S(1)}, bf16[128,2048]{1,0:T(8,128)(2,1)S(1)}, u32[]{:S(2)}, u32[]{:S(2)}) collective-permute-start(bf16[128,2048]{1,0:T(8,128)(2,1)S(1)} %get-tuple-element.172), channel_id=1, source_target_pairs={{0,4},{4,0},{8,12},{12,8},{16,20},{20,16},{24,28},{28,24},{1,5},{5... | collective-permute-start | bytes 1572872 | tf_op jit(solution)/shard_map/ppermute | solution.py:35
  131.2 16.8 %collective-permute-start.27 = (bf16[128,2048]{1,0:T(8,128)(2,1)S(1)}, bf16[128,2048]{1,0:T(8,128)(2,1)S(1)}, u32[]{:S(2)}, u32[]{:S(2)}) collective-permute-start(bf16[128,2048]{1,0:T(8,128)(2,1)S(1)} %add_convert_fusion.8), channel_id=1, source_target_pairs={{0,8},{4,12},{8,16},{12,20},{16,24},{20,28},{24,0},{28,4},{1,9},{5... | collective-permute-start | bytes 1572872 | tf_op jit(solution)/shard_map/ppermute | solution.py:32
  133.0 23.8 %collective-permute-start.25 = (bf16[128,2048]{1,0:T(8,128)(2,1)S(1)}, bf16[128,2048]{1,0:T(8,128)(2,1)S(1)}, u32[]{:S(2)}, u32[]{:S(2)}) collective-permute-start(bf16[128,2048]{1,0:T(8,128)(2,1)S(1)} %add_convert_fusion.9), channel_id=1, source_target_pairs={{0,24},{4,28},{8,0},{12,4},{16,8},{20,12},{24,16},{28,20},{1,25},{... | collective-permute-start | bytes 1572872 | tf_op jit(solution)/shard_map/ppermute | solution.py:32
  135.4 24.4 %collective-permute-start.20 = (f32[1,128]{1,0:T(1,128)S(1)}, f32[1,128]{1,0:T(1,128)S(1)}, u32[]{:S(2)}, u32[]{:S(2)}) collective-permute-start(f32[1,128]{1,0:T(1,128)S(1)} %add.277), channel_id=1, source_target_pairs={{0,2},{1,3},{2,0},{3,1},{4,6},{5,7},{6,4},{7,5},{8,10},{9,11},{10,... | collective-permute-start | bytes 1544 | tf_op jit(solution)/shard_map/ppermute | solution.py:38
where the time goes:
time: 164 us; the launch traced here: 163 us
  waiting for transfers between devices  56 us (34%)
  matrix products  41.9 us (26%)
  starting transfers between devices  33.2 us (20%)
  other arithmetic  15.9 us (10%)
  local copies, waits for them, and re-layouts  14.4 us (9%)
    dot_general x24, matrix products, dot(): lax.dot_general(a, b, (((ca,), (cb,)), ((), ())), preferred_element_type=...  41.9 us
    ppermute x10, waiting for transfers between devices, ring(): return lax.ppermute(value, 'expert', pairs)  29 us
    ppermute x11, waiting for transfers between devices, cross(): return lax.ppermute(value, 'expert', [(i, i ^ 1) for i in range(devices)])  23.2 us
    ppermute x10, starting transfers between devices, ring(): return lax.ppermute(value, 'expert', pairs)  16 us
    ppermute x11, starting transfers between devices, cross(): return lax.ppermute(value, 'expert', [(i, i ^ 1) for i in range(devices)])  12.7 us
    unnamed x47, local copies, waits for them, and re-layouts  8.03 us
    ppermute x9, starting transfers between devices, swap(): return lax.ppermute(value, 'dp', [(i, i ^ bit) for i in range(groups)])  4.54 us
    ppermute x9, waiting for transfers between devices, swap(): return lax.ppermute(value, 'dp', [(i, i ^ bit) for i in range(groups)])  3.81 us
  transfers between devices with their start and end apart: 30, of which 18 were waited for; matrix products, arithmetic and copies ran while one was open for 41% of the time, Pallas kernels for 0%

commit v1 on v0

--- a/solution.py
+++ b/solution.py
@@ -184,16 +184,14 @@
     far_gate, late_delta = tie(far_gate, late_delta)
     far_up = chunk(0, late_delta, 1)
     flying_up = swap(far_up, 1)
-    far_up, late_delta, flying_gate, flying_load = tie(far_up, late_delta, flying_gate, flying_load)
-    load = load + flying_load
-    flying_load = swap(load, 2)
+    all_down = (dot(late_hidden, late_grads, 0, 0) + early_down.astype(F32)).astype(BF)
+    far_up, late_delta, flying_gate, all_down = tie(far_up, late_delta, flying_gate, all_down)
     gate_sum = chunk(1, late_delta, 0, flying_gate)
     flying_gate = swap(gate_sum, 2)
     gate_sum, late_hidden, late_grads, late_delta, value = tie(
         gate_sum, late_hidden, late_grads, late_delta, crossed[middle_step]
     )
     minus = ring(add(own[middle_step], value), outer - 1)
-    all_down = (dot(late_hidden, late_grads, 0, 0) + early_down.astype(F32)).astype(BF)
     all_down = all_down.reshape(local_experts, groups, hidden // groups, width)
     down = [lax.dynamic_index_in_dim(all_down, c, 1, keepdims=False) for c in chunk_order]
     flying_down = swap(down[0], 1)
@@ -202,7 +200,11 @@
     up_sum, flying_down, delta, late_delta = tie(up_sum, flying_down, delta, late_delta)
     message = joined(up_sum, add(down[1], flying_down))
     flying_far = swap(message, 2)
-    message, delta, late_delta, near_down, first_other = tie(message, delta, late_delta, down[2], other[0])
+    message, delta, late_delta, near_down, first_other, flying_load = tie(
+        message, delta, late_delta, down[2], other[0], flying_load
+    )
+    load = load + flying_load
+    flying_load = swap(load, 2)
     last_partial = partial_input(delta)
     crossed[outer - 1] = cross(last_partial)
     near_sum = swap(whole_chunk(2, late_delta), 1)

time: 164 us -> 160 us (0.976)
  waiting for transfers between devices: 56 us -> 52.3 us
    ppermute x9, waiting for transfers between devices: 3.81 us -> 1.76 us  [swap(): return lax.ppermute(value, 'dp', [(i, i ^ bit) for i in range(groups)])]
    ppermute x11, waiting for transfers between devices: 23.2 us -> 21.4 us  [cross(): return lax.ppermute(value, 'expert', [(i, i ^ 1) for i in range(devices)])]
  transfers between devices with their start and end apart: 30 -> 30, of which waited for: 18 -> 16; matrix products, arithmetic and copies ran while one was open for 41% -> 42% of each run, Pallas kernels for 0% -> 0%
where the time goes in v1:
time: 160 us; the launch traced here: 159 us
  waiting for transfers between devices  52.3 us (33%)
  matrix products  41.9 us (26%)
  starting transfers between devices  33.2 us (21%)
  other arithmetic  15.7 us (10%)
  local copies, waits for them, and re-layouts  14.8 us (9%)
    dot_general x24, matrix products, dot(): lax.dot_general(a, b, (((ca,), (cb,)), ((), ())), preferred_element_type=...  41.9 us
    ppermute x10, waiting for transfers between devices, ring(): return lax.ppermute(value, 'expert', pairs)  29.1 us
    ppermute x11, waiting for transfers between devices, cross(): return lax.ppermute(value, 'expert', [(i, i ^ 1) for i in range(devices)])  21.4 us
    ppermute x10, starting transfers between devices, ring(): return lax.ppermute(value, 'expert', pairs)  15.9 us
    ppermute x11, starting transfers between devices, cross(): return lax.ppermute(value, 'expert', [(i, i ^ 1) for i in range(devices)])  12.8 us
    unnamed x47, local copies, waits for them, and re-layouts  8.09 us
    ppermute x9, starting transfers between devices, swap(): return lax.ppermute(value, 'dp', [(i, i ^ bit) for i in range(groups)])  4.47 us
    squeeze x1, local copies, waits for them, and re-layouts, shards(): up_weight[e]  3.46 us
  transfers between devices with their start and end apart: 30, of which 16 were waited for; matrix products, arithmetic and copies ran while one was open for 42% of the time, Pallas kernels for 0%

profile of v1, /device:TPU:0, one launch (start us, length us, event | category | flops | bytes accessed | tf_op | source)
XLA Modules:
  0.0 159.4 jit_solution(14108485633678099896)
XLA Ops:
  0.6 3.0 %collective-permute-start.1 = (bf16[128,2048]{1,0:T(8,128)(2,1)}, bf16[128,2048]{1,0:T(8,128)(2,1)}, u32[]{:S(2)}, u32[]{:S(2)}) collective-permute-start(bf16[128,2048]{1,0:T(8,128)(2,1)} %param.7), channel_id=1, source_target_pairs={{0,4},{4,0},{8,12},{12,8},{16,20},{20,16},{24,28},{28,24},{1,5},{5... | collective-permute-start | bytes 1572872 | tf_op jit(solution)/shard_map/ppermute | solution.py:35
  3.7 1.6 collective-permute-start
  7.2 1.9 %pad_maximum_fusion.19 = bf16[128,2176]{1,0:T(8,128)(2,1)} fusion(bf16[128,128]{1,0:T(8,128)(2,1)S(1)} %select_reduce_fusion, bf16[128,2048]{1,0:T(8,128)(2,1)} %param.8), kind=kLoop, calls=%fused_computation.107 | loop fusion | flops 1114112 | bytes 1114112 | tf_op jit(solution)/shard_map/concatenate | solution.py:47
  9.6 1.6 collective-permute-start.4
  11.2 3.5 %slice_bitcast_fusion.1 = (bf16[2048,384]{1,0:T(8,128)(2,1)S(1)}, bf16[2048,384]{1,0:T(8,128)(2,1)S(1)}, bf16[2048,384]{1,0:T(8,128)(2,1)S(1)}, bf16[2048,384]{1,0:T(8,128)(2,1)S(1)}) fusion(bf16[2,2048,384]{2,1,0:T(8,128)(2,1)} %param.12, bf16[2,2048,384]{2,1,0:T(8,128)(2,1)} %param.11), kind=kLoop, calls=%fused_computation.38 | loop fusion | bytes 12582912 | tf_op jit(solution)/shard_map/squeeze | solution.py:50
  14.6 3.1 %pad_maximum_fusion = bf16[2048,1536]{1,0:T(8,128)(2,1)} fusion(bf16[2048,384]{1,0:T(8,128)(2,1)S(1)} %get-tuple-element.201, bf16[2048,384]{1,0:T(8,128)(2,1)S(1)} %get-tuple-element.200, bf16[2048,384]{1,0:T(8,128)(2,1)S(1)} %get-tuple-element.260, bf16[2048,384]{1,0:T(8,128)(2,1)S(1)} %get-tuple-element.261), kind=kLoop, calls=%fused_computation | loop fusion | flops 25165824 | bytes 12582912 | tf_op jit(solution)/shard_map/concatenate | solution.py:49
  17.8 1.1 dynamic-slice_dynamic-update-slice_fusion.4
  19.0 1.1 constant_dynamic-update-slice_fusion.4
  20.6 1.1 collective-permute-start.3
  21.7 1.6 collective-permute-start.2
  23.3 1.1 dynamic-slice_dynamic-update-slice_fusion.3
  24.4 1.1 dynamic-slice_dynamic-update-slice_fusion.2
  25.5 5.0 %fusion.5 = f32[384,1536]{1,0:T(8,128)S(1)} fusion(bf16[2048,1536]{1,0:T(8,128)(2,1)} %pad_maximum_fusion, bf16[128,2048]{1,0:T(8,128)(2,1)} %collective-permute-done.1, bf16[128,2048]{1,0:T(8,128)(2,1)} %collective-permute-done, bf16[128,2048]{1,0:T(8,128)(2,1)S(1)} %copy-done.5), kind=kOutput, calls=%fused_computation.21 | convolution fusion | flops 2420637696 | bytes 10223616 | tf_op jit(solution)/shard_map/dot_general | solution.py:12
  30.6 2.0 %collective-permute-done.4 = bf16[128,2176]{1,0:T(8,128)(2,1)} collective-permute-done((bf16[128,2176]{1,0:T(8,128)(2,1)}, bf16[128,2176]{1,0:T(8,128)(2,1)}, u32[]{:S(2)}, u32[]{:S(2)}) %collective-permute-start.4) | collective-permute-done | bytes 557088 | tf_op jit(solution)/shard_map/ppermute | solution.py:32
  33.7 1.1 slice_dynamic-update-slice_fusion.3
  35.7 1.1 slice_dynamic-update-slice_fusion.2
  36.8 0.9 fusion.53
  38.0 3.3 %multiply_convert_fusion.1 = (bf16[384,768]{1,0:T(8,128)(2,1)S(1)}, bf16[384,768]{1,0:T(8,128)(2,1)S(1)}, bf16[384,768]{1,0:T(8,128)(2,1)S(1)}) fusion(f32[384,1536]{1,0:T(8,128)S(1)} %fusion.5, f32[384,384]{1,0:T(8,128)S(1)} %broadcast_in_dim.117, f32[384,384]{1,0:T(8,128)S(1)} %broadcast_in_dim.115, bf16[768,2048]{1,0:T(8,128)(2,1)S(1)} %bitcast.64, ...), kind=kOutput, calls=%fused_computation.52 | convolution fusion | flops 1219559424 | bytes 10125312 | tf_op jit(solution)/shard_map/dot_general | solution.py:12
  41.3 2.6 %convolution_convert_fusion.5 = bf16[384,2048]{1,0:T(8,128)(2,1)S(1)} fusion(bf16[2048,1536]{1,0:T(8,128)(2,1)S(1)} %bitcast.69, bf16[384,768]{1,0:T(8,128)(2,1)S(1)} %get-tuple-element.193, bf16[384,768]{1,0:T(8,128)(2,1)S(1)} %get-tuple-element.192), kind=kOutput, calls=%fused_computation.12 | convolution fusion | flops 2419064832 | bytes 9043968 | tf_op jit(solution)/shard_map/dot_general | solution.py:12
  44.2 1.8 %collective-permute-start.7 = (bf16[128,2048]{1,0:T(8,128)(2,1)S(1)}, bf16[128,2048]{1,0:T(8,128)(2,1)S(1)}, u32[]{:S(2)}, u32[]{:S(2)}) collective-permute-start(bf16[128,2048]{1,0:T(8,128)(2,1)S(1)} %collective-permute-done.2), channel_id=1, source_target_pairs={{0,4},{4,0},{8,12},{12,8},{16,20},{20,16},{24,28},{28,24},{1,5},{5... | collective-permute-start | bytes 1572872 | tf_op jit(solution)/shard_map/ppermute | solution.py:35
  46.0 1.3 collective-permute-start.6
  47.5 1.8 %fusion.20 = f32[256,1536]{1,0:T(8,128)S(1)} fusion(bf16[2048,1536]{1,0:T(8,128)(2,1)S(1)} %bitcast.69, bf16[128,2048]{1,0:T(8,128)(2,1)S(1)} %collective-permute-done.3, bf16[128,2048]{1,0:T(8,128)(2,1)S(1)} %collective-permute-done.2), kind=kOutput, calls=%fused_computation.57 | convolution fusion | flops 1612709888 | bytes 8912896 | tf_op jit(solution)/shard_map/dot_general | solution.py:12
  49.3 2.4 %collective-permute-done.9 = bf16[128,2176]{1,0:T(8,128)(2,1)S(1)} collective-permute-done((bf16[128,2176]{1,0:T(8,128)(2,1)}, bf16[128,2176]{1,0:T(8,128)(2,1)S(1)}, u32[]{:S(2)}, u32[]{:S(2)}) %collective-permute-start.9) | collective-permute-done | bytes 557088 | tf_op jit(solution)/shard_map/ppermute | solution.py:35
  51.7 3.9 %collective-permute-done.8 = bf16[128,2176]{1,0:T(8,128)(2,1)S(1)} collective-permute-done((bf16[128,2176]{1,0:T(8,128)(2,1)}, bf16[128,2176]{1,0:T(8,128)(2,1)S(1)}, u32[]{:S(2)}, u32[]{:S(2)}) %collective-permute-start.8) | collective-permute-done | bytes 557088 | tf_op jit(solution)/shard_map/ppermute | solution.py:32
  56.5 1.4 multiply_convert_fusion.9
  57.9 1.8 %convolution_convert_fusion.7 = bf16[256,2048]{1,0:T(8,128)(2,1)S(1)} fusion(bf16[2048,1536]{1,0:T(8,128)(2,1)S(1)} %bitcast.69, bf16[256,768]{1,0:T(8,128)(2,1)S(1)} %get-tuple-element.205, bf16[256,768]{1,0:T(8,128)(2,1)S(1)} %get-tuple-element.204), kind=kOutput, calls=%fused_computation.14 | convolution fusion | flops 1612709888 | bytes 8126464 | tf_op jit(solution)/shard_map/dot_general | solution.py:12
  60.0 3.0 %collective-permute-done.7 = bf16[128,2048]{1,0:T(8,128)(2,1)S(1)} collective-permute-done((bf16[128,2048]{1,0:T(8,128)(2,1)S(1)}, bf16[128,2048]{1,0:T(8,128)(2,1)S(1)}, u32[]{:S(2)}, u32[]{:S(2)}) %collective-permute-start.7) | collective-permute-done | bytes 524320 | tf_op jit(solution)/shard_map/ppermute | solution.py:35
  63.0 3.9 %collective-permute-done.6 = bf16[128,2048]{1,0:T(8,128)(2,1)S(1)} collective-permute-done((bf16[128,2048]{1,0:T(8,128)(2,1)S(1)}, bf16[128,2048]{1,0:T(8,128)(2,1)S(1)}, u32[]{:S(2)}, u32[]{:S(2)}) %collective-permute-start.6) | collective-permute-done | bytes 524320 | tf_op jit(solution)/shard_map/ppermute | solution.py:32
  67.3 1.4 convolution_convert_fusion.1
  68.7 1.4 convolution_convert_fusion.2
  70.2 1.4 convolution_convert_fusion.3
  71.6 1.4 convolution_convert_fusion.4
  73.0 4.0 %convolution_convert_fusion = bf16[768,2048]{1,0:T(8,128)(2,1)} fusion(bf16[640,2048]{1,0:T(8,128)(2,1)S(1)} %slice_dynamic-update-slice_fusion, bf16[256,768]{1,0:T(8,128)(2,1)S(1)} %get-tuple-element.118, bf16[384,768]{1,0:T(8,128)(2,1)S(1)} %get-tuple-element.117), kind=kOutput, calls=%fused_computation.2 | convolution fusion | flops 2016804864 | bytes 6750208 | tf_op jit(solution)/shard_map/dot_general | solution.py:12
  77.1 2.3 %collective-permute-start.10 = (bf16[128,2176]{1,0:T(8,128)(2,1)}, bf16[128,2176]{1,0:T(8,128)(2,1)S(1)}, u32[]{:S(2)}, u32[]{:S(2)}) collective-permute-start(bf16[128,2176]{1,0:T(8,128)(2,1)} %collective-permute-done.5), channel_id=1, source_target_pairs={{0,24},{4,28},{8,0},{12,4},{16,8},{20,12},{24,16},{28,20},{1,25},{... | collective-permute-start | bytes 1671176 | tf_op jit(solution)/shard_map/ppermute | solution.py:32
  79.4 1.8 %fusion.24 = f32[256,1536]{1,0:T(8,128)S(1)} fusion(bf16[2048,1536]{1,0:T(8,128)(2,1)S(1)} %bitcast.69, bf16[128,2048]{1,0:T(8,128)(2,1)S(1)} %collective-permute-done.7, bf16[128,2048]{1,0:T(8,128)(2,1)S(1)} %collective-permute-done.6), kind=kOutput, calls=%fused_computation.61 | convolution fusion | flops 1612709888 | bytes 8912896 | tf_op jit(solution)/shard_map/dot_general | solution.py:12
  81.7 1.4 multiply_convert_fusion.7
  83.2 1.8 %convolution_convert_fusion.6 = bf16[256,2048]{1,0:T(8,128)(2,1)S(1)} fusion(bf16[2048,1536]{1,0:T(8,128)(2,1)S(1)} %bitcast.69, bf16[256,768]{1,0:T(8,128)(2,1)S(1)} %get-tuple-element.203, bf16[256,768]{1,0:T(8,128)(2,1)S(1)} %get-tuple-element.202), kind=kOutput, calls=%fused_computation.13 | convolution fusion | flops 1612709888 | bytes 8126464 | tf_op jit(solution)/shard_map/dot_general | solution.py:12
  85.3 1.8 %collective-permute-start.16 = (bf16[128,2048]{1,0:T(8,128)(2,1)S(1)}, bf16[128,2048]{1,0:T(8,128)(2,1)S(1)}, u32[]{:S(2)}, u32[]{:S(2)}) collective-permute-start(bf16[128,2048]{1,0:T(8,128)(2,1)S(1)} %get-tuple-element.133), channel_id=1, source_target_pairs={{0,4},{4,0},{8,12},{12,8},{16,20},{20,16},{24,28},{28,24},{1,5},{5... | collective-permute-start | bytes 1572872 | tf_op jit(solution)/shard_map/ppermute | solution.py:35
  87.3 1.0 fusion.73
  88.3 1.3 collective-permute-done.10
  90.0 1.3 multiply_convert_fusion.11
  93.8 1.9 %add_convert_fusion = bf16[768,2048]{1,0:T(8,128)(2,1)S(1)} fusion(bf16[768,2048]{1,0:T(8,128)(2,1)S(1)} %copy-done.6, bf16[128,768]{1,0:T(8,128)(2,1)S(1)} %get-tuple-element.227, bf16[256,768]{1,0:T(8,128)(2,1)S(1)} %get-tuple-element.128, bf16[128,2048]{1,0:T(8,128)(2,1)S(1)} %slice-done.4, bf16[128,2048]{1,0:T(8,128)(2,1)S(1)} %slice-done.2, ...), kind=kOutput, calls=%fused_computation.1 | convolution fusion | flops 1218576384 | bytes 8454144 | tf_op jit(solution)/shard_map/dot_general | solution.py:12
  97.1 1.4 collective-permute-done.16
  100.0 1.3 fusion.1
  101.4 1.5 collective-permute-start.22
  102.9 1.5 collective-permute-start.29
  104.5 3.6 %collective-permute-start.21 = (bf16[128,2048]{1,0:T(8,128)(2,1)S(1)}, bf16[128,2048]{1,0:T(8,128)(2,1)S(1)}, u32[]{:S(2)}, u32[]{:S(2)}) collective-permute-start(bf16[128,2048]{1,0:T(8,128)(2,1)S(1)} %add_convert_fusion.10), channel_id=1, source_target_pairs={{0,24},{4,28},{8,0},{12,4},{16,8},{20,12},{24,16},{28,20},{1,25},{... | collective-permute-start | bytes 1572872 | tf_op jit(solution)/shard_map/ppermute | solution.py:32
  108.2 2.1 %convolution_convert_fusion.8 = bf16[128,2048]{1,0:T(8,128)(2,1)S(1)} fusion(bf16[128,1536]{1,0:T(8,128)(2,1)S(1)} %pad_maximum_fusion.27, bf16[2048,1536]{1,0:T(8,128)(2,1)S(1)} %bitcast.69), kind=kOutput, calls=%fused_computation.15 | convolution fusion | flops 805568512 | bytes 7208960 | tf_op jit(solution)/shard_map/dot_general | solution.py:12
  111.4 1.2 fusion.2
  113.0 3.2 %collective-permute-done.22 = bf16[128,2048]{1,0:T(8,128)(2,1)S(1)} collective-permute-done((bf16[128,2048]{1,0:T(8,128)(2,1)S(1)}, bf16[128,2048]{1,0:T(8,128)(2,1)S(1)}, u32[]{:S(2)}, u32[]{:S(2)}) %collective-permute-start.22) | collective-permute-done | bytes 524320 | tf_op jit(solution)/shard_map/ppermute | solution.py:35
  116.2 1.4 collective-permute-start.28
  117.6 2.4 %collective-permute-done.21 = bf16[128,2048]{1,0:T(8,128)(2,1)S(1)} collective-permute-done((bf16[128,2048]{1,0:T(8,128)(2,1)S(1)}, bf16[128,2048]{1,0:T(8,128)(2,1)S(1)}, u32[]{:S(2)}, u32[]{:S(2)}) %collective-permute-start.21) | collective-permute-done | bytes 524320 | tf_op jit(solution)/shard_map/ppermute | solution.py:32
  120.0 7.4 %collective-permute-done.26 = bf16[128,2048]{1,0:T(8,128)(2,1)S(1)} collective-permute-done((bf16[128,2048]{1,0:T(8,128)(2,1)S(1)}, bf16[128,2048]{1,0:T(8,128)(2,1)S(1)}, u32[]{:S(2)}, u32[]{:S(2)}) %collective-permute-start.26) | collective-permute-done | bytes 524320 | tf_op jit(solution)/shard_map/ppermute | solution.py:35
  127.5 1.5 collective-permute-start.27
  129.3 2.4 %collective-permute-start.25 = (bf16[128,2048]{1,0:T(8,128)(2,1)S(1)}, bf16[128,2048]{1,0:T(8,128)(2,1)S(1)}, u32[]{:S(2)}, u32[]{:S(2)}) collective-permute-start(bf16[128,2048]{1,0:T(8,128)(2,1)S(1)} %add_convert_fusion.9), channel_id=1, source_target_pairs={{0,24},{4,28},{8,0},{12,4},{16,8},{20,12},{24,16},{28,20},{1,25},{... | collective-permute-start | bytes 1572872 | tf_op jit(solution)/shard_map/ppermute | solution.py:32
  131.7 1.4 collective-permute-start.20
  133.4 1.0 pad_maximum_fusion.16
  134.4 3.8 %collective-permute-done.28 = bf16[128,2048]{1,0:T(8,128)(2,1)S(1)} collective-permute-done((bf16[128,2048]{1,0:T(8,128)(2,1)S(1)}, bf16[128,2048]{1,0:T(8,128)(2,1)S(1)}, u32[]{:S(2)}, u32[]{:S(2)}) %collective-permute-start.28) | collective-permute-done | bytes 524320 | tf_op jit(solution)/shard_map/ppermute | solution.py:35
  138.2 6.1 %collective-permute-done.27 = bf16[128,2048]{1,0:T(8,128)(2,1)S(1)} collective-permute-done((bf16[128,2048]{1,0:T(8,128)(2,1)S(1)}, bf16[128,2048]{1,0:T(8,128)(2,1)S(1)}, u32[]{:S(2)}, u32[]{:S(2)}) %collective-permute-start.27) | collective-permute-done | bytes 524320 | tf_op jit(solution)/shard_map/ppermute | solution.py:32
  144.3 9.1 %collective-permute-done.25 = bf16[128,2048]{1,0:T(8,128)(2,1)S(1)} collective-permute-done((bf16[128,2048]{1,0:T(8,128)(2,1)S(1)}, bf16[128,2048]{1,0:T(8,128)(2,1)S(1)}, u32[]{:S(2)}, u32[]{:S(2)}) %collective-permute-start.25) | collective-permute-done | bytes 524320 | tf_op jit(solution)/shard_map/ppermute | solution.py:32
  153.4 1.1 add_convert_fusion.7
  154.5 1.7 %collective-permute-done.20 = f32[1,128]{1,0:T(1,128)S(1)} collective-permute-done((f32[1,128]{1,0:T(1,128)S(1)}, f32[1,128]{1,0:T(1,128)S(1)}, u32[]{:S(2)}, u32[]{:S(2)}) %collective-permute-start.20) | collective-permute-done | bytes 544 | tf_op jit(solution)/shard_map/ppermute | solution.py:38
  157.2 1.0 pad_maximum_fusion.17
  158.2 1.2 fusion.12
  (141 shorter events, 16.9 us)
Async XLA Ops:
  0.6 37.0 %copy-start = (bf16[2,384,2048]{2,1,0:T(8,128)(2,1)S(1)}, bf16[2,384,2048]{2,1,0:T(8,128)(2,1)}, u32[]{:S(2)}) copy-start(bf16[2,384,2048]{2,1,0:T(8,128)(2,1)} %param.13) | copy-start | bytes 9437188
  0.6 19.5 %collective-permute-start.1 = (bf16[128,2048]{1,0:T(8,128)(2,1)}, bf16[128,2048]{1,0:T(8,128)(2,1)}, u32[]{:S(2)}, u32[]{:S(2)}) collective-permute-start(bf16[128,2048]{1,0:T(8,128)(2,1)} %param.7), channel_id=1, source_target_pairs={{0,4},{4,0},{8,12},{12,8},{16,20},{20,16},{24,28},{28,24},{1,5},{5... | collective-permute-start | bytes 1572872 | tf_op jit(solution)/shard_map/ppermute | solution.py:35
  3.7 17.0 %collective-permute-start = (bf16[128,2048]{1,0:T(8,128)(2,1)}, bf16[128,2048]{1,0:T(8,128)(2,1)}, u32[]{:S(2)}, u32[]{:S(2)}) collective-permute-start(bf16[128,2048]{1,0:T(8,128)(2,1)} %param.7), channel_id=1, source_target_pairs={{0,8},{4,12},{8,16},{12,20},{16,24},{20,28},{24,0},{28,4},{1,9},{5... | collective-permute-start | bytes 1572872 | tf_op jit(solution)/shard_map/ppermute | solution.py:32
  9.1 21.5 %collective-permute-start.5 = (bf16[128,2176]{1,0:T(8,128)(2,1)}, bf16[128,2176]{1,0:T(8,128)(2,1)}, u32[]{:S(2)}, u32[]{:S(2)}) collective-permute-start(bf16[128,2176]{1,0:T(8,128)(2,1)} %pad_maximum_fusion.19), channel_id=1, source_target_pairs={{0,4},{4,0},{8,12},{12,8},{16,20},{20,16},{24,28},{28,24},{1,5},{5... | collective-permute-start | bytes 1671176 | tf_op jit(solution)/shard_map/ppermute | solution.py:35
  9.6 23.0 %collective-permute-start.4 = (bf16[128,2176]{1,0:T(8,128)(2,1)}, bf16[128,2176]{1,0:T(8,128)(2,1)}, u32[]{:S(2)}, u32[]{:S(2)}) collective-permute-start(bf16[128,2176]{1,0:T(8,128)(2,1)} %pad_maximum_fusion.19), channel_id=1, source_target_pairs={{0,8},{4,12},{8,16},{12,20},{16,24},{20,28},{24,0},{28,4},{1,9},{5... | collective-permute-start | bytes 1671176 | tf_op jit(solution)/shard_map/ppermute | solution.py:32
  18.9 6.6 %copy-start.5 = (bf16[128,2048]{1,0:T(8,128)(2,1)S(1)}, bf16[128,2048]{1,0:T(8,128)(2,1)}, u32[]{:S(2)}) copy-start(bf16[128,2048]{1,0:T(8,128)(2,1)} %param.7) | copy-start | bytes 1572868
  20.6 23.6 %collective-permute-start.3 = (bf16[128,2048]{1,0:T(8,128)(2,1)}, bf16[128,2048]{1,0:T(8,128)(2,1)S(1)}, u32[]{:S(2)}, u32[]{:S(2)}) collective-permute-start(bf16[128,2048]{1,0:T(8,128)(2,1)} %collective-permute-done), channel_id=1, source_target_pairs={{0,4},{4,0},{8,12},{12,8},{16,20},{20,16},{24,28},{28,24},{1,5},{5... | collective-permute-start | bytes 1572872 | tf_op jit(solution)/shard_map/ppermute | solution.py:35
  21.7 22.5 %collective-permute-start.2 = (bf16[128,2048]{1,0:T(8,128)(2,1)}, bf16[128,2048]{1,0:T(8,128)(2,1)S(1)}, u32[]{:S(2)}, u32[]{:S(2)}) collective-permute-start(bf16[128,2048]{1,0:T(8,128)(2,1)} %collective-permute-done), channel_id=1, source_target_pairs={{0,8},{4,12},{8,16},{12,20},{16,24},{20,28},{24,0},{28,4},{1,9},{5... | collective-permute-start | bytes 1572872 | tf_op jit(solution)/shard_map/ppermute | solution.py:32
  30.5 6.2 %copy-start.1 = (bf16[128,2048]{1,0:T(8,128)(2,1)S(1)}, bf16[128,2048]{1,0:T(8,128)(2,1)}, u32[]{:S(2)}) copy-start(bf16[128,2048]{1,0:T(8,128)(2,1)} %param.8) | copy-start | bytes 1572868
  33.3 18.4 %collective-permute-start.9 = (bf16[128,2176]{1,0:T(8,128)(2,1)}, bf16[128,2176]{1,0:T(8,128)(2,1)S(1)}, u32[]{:S(2)}, u32[]{:S(2)}) collective-permute-start(bf16[128,2176]{1,0:T(8,128)(2,1)} %collective-permute-done.4), channel_id=1, source_target_pairs={{0,4},{4,0},{8,12},{12,8},{16,20},{20,16},{24,28},{28,24},{1,5},{5... | collective-permute-start | bytes 1671176 | tf_op jit(solution)/shard_map/ppermute | solution.py:35
  33.7 21.9 %collective-permute-start.8 = (bf16[128,2176]{1,0:T(8,128)(2,1)}, bf16[128,2176]{1,0:T(8,128)(2,1)S(1)}, u32[]{:S(2)}, u32[]{:S(2)}) collective-permute-start(bf16[128,2176]{1,0:T(8,128)(2,1)} %collective-permute-done.4), channel_id=1, source_target_pairs={{0,8},{4,12},{8,16},{12,20},{16,24},{20,28},{24,0},{28,4},{1,9},{5... | collective-permute-start | bytes 1671176 | tf_op jit(solution)/shard_map/ppermute | solution.py:32
  37.8 3.4 %slice-start = ((s8[6291456]{0:T(1024)(128)(4,1)}), s8[4194304]{0:T(1024)(128)(4,1)S(1)}, s32[]{:S(2)}) async-start(s8[6291456]{0:T(1024)(128)(4,1)} %bitcast.68), calls=%async_computation | async-start | bytes 8388608
  37.9 3.3 %slice-start.1 = ((s8[6291456]{0:T(1024)(128)(4,1)}), s8[2097152]{0:T(1024)(128)(4,1)S(1)}, s32[]{:S(2)}) async-start(s8[6291456]{0:T(1024)(128)(4,1)} %bitcast.68), calls=%async_computation.1 | async-start | bytes 4194304
  44.2 18.8 %collective-permute-start.7 = (bf16[128,2048]{1,0:T(8,128)(2,1)S(1)}, bf16[128,2048]{1,0:T(8,128)(2,1)S(1)}, u32[]{:S(2)}, u32[]{:S(2)}) collective-permute-start(bf16[128,2048]{1,0:T(8,128)(2,1)S(1)} %collective-permute-done.2), channel_id=1, source_target_pairs={{0,4},{4,0},{8,12},{12,8},{16,20},{20,16},{24,28},{28,24},{1,5},{5... | collective-permute-start | bytes 1572872 | tf_op jit(solution)/shard_map/ppermute | solution.py:35
  46.0 20.9 %collective-permute-start.6 = (bf16[128,2048]{1,0:T(8,128)(2,1)S(1)}, bf16[128,2048]{1,0:T(8,128)(2,1)S(1)}, u32[]{:S(2)}, u32[]{:S(2)}) collective-permute-start(bf16[128,2048]{1,0:T(8,128)(2,1)S(1)} %collective-permute-done.2), channel_id=1, source_target_pairs={{0,8},{4,12},{8,16},{12,20},{16,24},{20,28},{24,0},{28,4},{1,9},{5... | collective-permute-start | bytes 1572872 | tf_op jit(solution)/shard_map/ppermute | solution.py:32
  55.6 25.6 %collective-permute-start.13 = (bf16[128,2176]{1,0:T(8,128)(2,1)S(1)}, bf16[128,2176]{1,0:T(8,128)(2,1)S(1)}, u32[]{:S(2)}, u32[]{:S(2)}) collective-permute-start(bf16[128,2176]{1,0:T(8,128)(2,1)S(1)} %collective-permute-done.8), channel_id=1, source_target_pairs={{0,4},{4,0},{8,12},{12,8},{16,20},{20,16},{24,28},{28,24},{1,5},{5... | collective-permute-start | bytes 1671176 | tf_op jit(solution)/shard_map/ppermute | solution.py:35
  56.0 25.2 %collective-permute-start.12 = (bf16[128,2176]{1,0:T(8,128)(2,1)S(1)}, bf16[128,2176]{1,0:T(8,128)(2,1)S(1)}, u32[]{:S(2)}, u32[]{:S(2)}) collective-permute-start(bf16[128,2176]{1,0:T(8,128)(2,1)S(1)} %collective-permute-done.8), channel_id=1, source_target_pairs={{0,8},{4,12},{8,16},{12,20},{16,24},{20,28},{24,0},{28,4},{1,9},{5... | collective-permute-start | bytes 1671176 | tf_op jit(solution)/shard_map/ppermute | solution.py:32
  66.9 18.4 %collective-permute-start.11 = (bf16[128,2048]{1,0:T(8,128)(2,1)S(1)}, bf16[128,2048]{1,0:T(8,128)(2,1)S(1)}, u32[]{:S(2)}, u32[]{:S(2)}) collective-permute-start(bf16[128,2048]{1,0:T(8,128)(2,1)S(1)} %collective-permute-done.6), channel_id=1, source_target_pairs={{0,4},{4,0},{8,12},{12,8},{16,20},{20,16},{24,28},{28,24},{1,5},{5... | collective-permute-start | bytes 1572872 | tf_op jit(solution)/shard_map/ppermute | solution.py:35
  77.1 12.6 %collective-permute-start.10 = (bf16[128,2176]{1,0:T(8,128)(2,1)}, bf16[128,2176]{1,0:T(8,128)(2,1)S(1)}, u32[]{:S(2)}, u32[]{:S(2)}) collective-permute-start(bf16[128,2176]{1,0:T(8,128)(2,1)} %collective-permute-done.5), channel_id=1, source_target_pairs={{0,24},{4,28},{8,0},{12,4},{16,8},{20,12},{24,16},{28,20},{1,25},{... | collective-permute-start | bytes 1671176 | tf_op jit(solution)/shard_map/ppermute | solution.py:32
  81.2 3.8 %copy-start.2 = (bf16[128,2176]{1,0:T(8,128)(2,1)}, bf16[128,2176]{1,0:T(8,128)(2,1)S(1)}, u32[]{:S(2)}) copy-start(bf16[128,2176]{1,0:T(8,128)(2,1)S(1)} %collective-permute-done.13) | copy-start | bytes 1671172
  81.2 3.8 %copy-start.3 = (bf16[128,2176]{1,0:T(8,128)(2,1)}, bf16[128,2176]{1,0:T(8,128)(2,1)S(1)}, u32[]{:S(2)}) copy-start(bf16[128,2176]{1,0:T(8,128)(2,1)S(1)} %collective-permute-done.12) | copy-start | bytes 1671172
  85.3 13.2 %collective-permute-start.16 = (bf16[128,2048]{1,0:T(8,128)(2,1)S(1)}, bf16[128,2048]{1,0:T(8,128)(2,1)S(1)}, u32[]{:S(2)}, u32[]{:S(2)}) collective-permute-start(bf16[128,2048]{1,0:T(8,128)(2,1)S(1)} %get-tuple-element.133), channel_id=1, source_target_pairs={{0,4},{4,0},{8,12},{12,8},{16,20},{20,16},{24,28},{28,24},{1,5},{5... | collective-permute-start | bytes 1572872 | tf_op jit(solution)/shard_map/ppermute | solution.py:35
  89.6 1.6 %copy-start.4 = (bf16[128,2176]{1,0:T(8,128)(2,1)}, bf16[128,2176]{1,0:T(8,128)(2,1)S(1)}, u32[]{:S(2)}) copy-start(bf16[128,2176]{1,0:T(8,128)(2,1)S(1)} %collective-permute-done.10) | copy-start | bytes 1671172
  91.3 2.0 %copy-start.6 = (bf16[768,2048]{1,0:T(8,128)(2,1)S(1)}, bf16[768,2048]{1,0:T(8,128)(2,1)}, u32[]{:S(2)}) copy-start(bf16[768,2048]{1,0:T(8,128)(2,1)} %convolution_convert_fusion) | copy-start | bytes 9437188
  92.0 3.8 %collective-permute-start.15 = (bf16[512,768]{1,0:T(8,128)(2,1)S(1)}, bf16[512,768]{1,0:T(8,128)(2,1)S(1)}, u32[]{:S(2)}, u32[]{:S(2)}) collective-permute-start(bf16[512,768]{1,0:T(8,128)(2,1)S(1)} %add_convert_fusion.6), channel_id=1, source_target_pairs={{0,1},{1,0},{2,3},{3,2},{4,5},{5,4},{6,7},{7,6},{8,9},{9,8},{10,11... | collective-permute-start | bytes 2359304 | tf_op jit(solution)/shard_map/ppermute | solution.py:38
  92.1 1.4 slice-start.2
  92.1 1.6 slice-start.3
  92.1 1.7 %slice-start.4 = ((bf16[128,2176]{1,0:T(8,128)(2,1)}), bf16[128,2048]{1,0:T(8,128)(2,1)S(1)}, s32[]{:S(2)}) async-start(bf16[128,2176]{1,0:T(8,128)(2,1)} %copy-done.4), calls=%async_computation.4 | async-start | bytes 1048576 | tf_op jit(solution)/shard_map/slice | solution.py:56
  92.1 7.9 %collective-permute-start.19 = (f32[1,128]{1,0:T(1,128)S(1)}, f32[1,128]{1,0:T(1,128)S(1)}, u32[]{:S(2)}, u32[]{:S(2)}) collective-permute-start(f32[1,128]{1,0:T(1,128)S(1)} %add_bitcast_fusion), channel_id=1, source_target_pairs={{0,1},{1,0},{2,3},{3,2},{4,5},{5,4},{6,7},{7,6},{8,9},{9,8},{10,11... | collective-permute-start | bytes 1544 | tf_op jit(solution)/shard_map/ppermute | solution.py:38
  93.3 5.3 %collective-permute-start.14 = (bf16[512,768]{1,0:T(8,128)(2,1)S(1)}, bf16[512,768]{1,0:T(8,128)(2,1)S(1)}, u32[]{:S(2)}, u32[]{:S(2)}) collective-permute-start(bf16[512,768]{1,0:T(8,128)(2,1)S(1)} %add_convert_fusion.5), channel_id=1, source_target_pairs={{0,1},{1,0},{2,3},{3,2},{4,5},{5,4},{6,7},{7,6},{8,9},{9,8},{10,11... | collective-permute-start | bytes 2359304 | tf_op jit(solution)/shard_map/ppermute | solution.py:38
  96.0 3.4 %collective-permute-start.17 = (bf16[2,96,2048]{2,1,0:T(8,128)(2,1)S(1)}, bf16[2,96,2048]{2,1,0:T(8,128)(2,1)S(1)}, u32[]{:S(2)}, u32[]{:S(2)}) collective-permute-start(bf16[2,96,2048]{2,1,0:T(8,128)(2,1)S(1)} %get-tuple-element.197), channel_id=1, source_target_pairs={{0,1},{1,0},{2,3},{3,2},{4,5},{5,4},{6,7},{7,6},{8,9},{9,8},{10,11... | collective-permute-start | bytes 2359304 | tf_op jit(solution)/shard_map/ppermute | solution.py:38
  101.3 9.6 %collective-permute-start.23 = (bf16[512,1536]{1,0:T(8,128)(2,1)S(1)}, bf16[512,1536]{1,0:T(8,128)(2,1)S(1)}, u32[]{:S(2)}, u32[]{:S(2)}) collective-permute-start(bf16[512,1536]{1,0:T(8,128)(2,1)S(1)} %fusion.1), channel_id=1, source_target_pairs={{0,1},{1,0},{2,3},{3,2},{4,5},{5,4},{6,7},{7,6},{8,9},{9,8},{10,11... | collective-permute-start | bytes 4718600 | tf_op jit(solution)/shard_map/ppermute | solution.py:38
  101.4 14.8 %collective-permute-start.22 = (bf16[128,2048]{1,0:T(8,128)(2,1)S(1)}, bf16[128,2048]{1,0:T(8,128)(2,1)S(1)}, u32[]{:S(2)}, u32[]{:S(2)}) collective-permute-start(bf16[128,2048]{1,0:T(8,128)(2,1)S(1)} %get-tuple-element.149), channel_id=1, source_target_pairs={{0,4},{4,0},{8,12},{12,8},{16,20},{20,16},{24,28},{28,24},{1,5},{5... | collective-permute-start | bytes 1572872 | tf_op jit(solution)/shard_map/ppermute | solution.py:35
  102.9 28.9 %collective-permute-start.29 = (bf16[512,768]{1,0:T(8,128)(2,1)S(1)}, bf16[512,768]{1,0:T(8,128)(2,1)S(1)}, u32[]{:S(2)}, u32[]{:S(2)}) collective-permute-start(bf16[512,768]{1,0:T(8,128)(2,1)S(1)} %add_convert_fusion.4), channel_id=1, source_target_pairs={{0,2},{1,3},{2,0},{3,1},{4,6},{5,7},{6,4},{7,5},{8,10},{9,11},{10,... | collective-permute-start | bytes 2359304 | tf_op jit(solution)/shard_map/ppermute | solution.py:38
  104.4 5.9 %collective-permute-start.24 = (bf16[2,96,2048]{2,1,0:T(8,128)(2,1)S(1)}, bf16[2,96,2048]{2,1,0:T(8,128)(2,1)S(1)}, u32[]{:S(2)}, u32[]{:S(2)}) collective-permute-start(bf16[2,96,2048]{2,1,0:T(8,128)(2,1)S(1)} %get-tuple-element.154), channel_id=1, source_target_pairs={{0,1},{1,0},{2,3},{3,2},{4,5},{5,4},{6,7},{7,6},{8,9},{9,8},{10,11... | collective-permute-start | bytes 2359304 | tf_op jit(solution)/shard_map/ppermute | solution.py:38
  104.5 15.5 %collective-permute-start.21 = (bf16[128,2048]{1,0:T(8,128)(2,1)S(1)}, bf16[128,2048]{1,0:T(8,128)(2,1)S(1)}, u32[]{:S(2)}, u32[]{:S(2)}) collective-permute-start(bf16[128,2048]{1,0:T(8,128)(2,1)S(1)} %add_convert_fusion.10), channel_id=1, source_target_pairs={{0,24},{4,28},{8,0},{12,4},{16,8},{20,12},{24,16},{28,20},{1,25},{... | collective-permute-start | bytes 1572872 | tf_op jit(solution)/shard_map/ppermute | solution.py:32
  110.3 45.9 %collective-permute-start.18 = (bf16[3072,256]{1,0:T(8,128)(2,1)S(1)}, bf16[3072,256]{1,0:T(8,128)(2,1)S(1)}, u32[]{:S(2)}, u32[]{:S(2)}) collective-permute-start(bf16[3072,256]{1,0:T(8,128)(2,1)S(1)} %constant_dynamic-update-slice_fusion.7), channel_id=1, source_target_pairs={{0,2},{1,3},{2,0},{3,1},{4,6},{5,7},{6,4},{7,5},{8,10},{9,11},{10,... | collective-permute-start | bytes 4718600 | tf_op jit(solution)/shard_map/ppermute | solution.py:38
  110.9 16.5 %collective-permute-start.26 = (bf16[128,2048]{1,0:T(8,128)(2,1)S(1)}, bf16[128,2048]{1,0:T(8,128)(2,1)S(1)}, u32[]{:S(2)}, u32[]{:S(2)}) collective-permute-start(bf16[128,2048]{1,0:T(8,128)(2,1)S(1)} %convolution_convert_fusion.8), channel_id=1, source_target_pairs={{0,4},{4,0},{8,12},{12,8},{16,20},{20,16},{24,28},{28,24},{1,5},{5... | collective-permute-start | bytes 1572872 | tf_op jit(solution)/shard_map/ppermute | solution.py:35
  116.2 22.0 %collective-permute-start.28 = (bf16[128,2048]{1,0:T(8,128)(2,1)S(1)}, bf16[128,2048]{1,0:T(8,128)(2,1)S(1)}, u32[]{:S(2)}, u32[]{:S(2)}) collective-permute-start(bf16[128,2048]{1,0:T(8,128)(2,1)S(1)} %get-tuple-element.170), channel_id=1, source_target_pairs={{0,4},{4,0},{8,12},{12,8},{16,20},{20,16},{24,28},{28,24},{1,5},{5... | collective-permute-start | bytes 1572872 | tf_op jit(solution)/shard_map/ppermute | solution.py:35
  127.5 16.8 %collective-permute-start.27 = (bf16[128,2048]{1,0:T(8,128)(2,1)S(1)}, bf16[128,2048]{1,0:T(8,128)(2,1)S(1)}, u32[]{:S(2)}, u32[]{:S(2)}) collective-permute-start(bf16[128,2048]{1,0:T(8,128)(2,1)S(1)} %add_convert_fusion.8), channel_id=1, source_target_pairs={{0,8},{4,12},{8,16},{12,20},{16,24},{20,28},{24,0},{28,4},{1,9},{5... | collective-permute-start | bytes 1572872 | tf_op jit(solution)/shard_map/ppermute | solution.py:32
  129.3 24.0 %collective-permute-start.25 = (bf16[128,2048]{1,0:T(8,128)(2,1)S(1)}, bf16[128,2048]{1,0:T(8,128)(2,1)S(1)}, u32[]{:S(2)}, u32[]{:S(2)}) collective-permute-start(bf16[128,2048]{1,0:T(8,128)(2,1)S(1)} %add_convert_fusion.9), channel_id=1, source_target_pairs={{0,24},{4,28},{8,0},{12,4},{16,8},{20,12},{24,16},{28,20},{1,25},{... | collective-permute-start | bytes 1572872 | tf_op jit(solution)/shard_map/ppermute | solution.py:32
  131.7 24.5 %collective-permute-start.20 = (f32[1,128]{1,0:T(1,128)S(1)}, f32[1,128]{1,0:T(1,128)S(1)}, u32[]{:S(2)}, u32[]{:S(2)}) collective-permute-start(f32[1,128]{1,0:T(1,128)S(1)} %add.277), channel_id=1, source_target_pairs={{0,2},{1,3},{2,0},{3,1},{4,6},{5,7},{6,4},{7,5},{8,10},{9,11},{10,... | collective-permute-start | bytes 1544 | tf_op jit(solution)/shard_map/ppermute | solution.py:38

commit v2 on v1

--- a/solution.py
+++ b/solution.py
@@ -188,9 +188,7 @@
     far_up, late_delta, flying_gate, all_down = tie(far_up, late_delta, flying_gate, all_down)
     gate_sum = chunk(1, late_delta, 0, flying_gate)
     flying_gate = swap(gate_sum, 2)
-    gate_sum, late_hidden, late_grads, late_delta, value = tie(
-        gate_sum, late_hidden, late_grads, late_delta, crossed[middle_step]
-    )
+    gate_sum, value = tie(gate_sum, crossed[middle_step])
     minus = ring(add(own[middle_step], value), outer - 1)
     all_down = all_down.reshape(local_experts, groups, hidden // groups, width)
     down = [lax.dynamic_index_in_dim(all_down, c, 1, keepdims=False) for c in chunk_order]

time: 160 us -> 172 us (1.075)
  waiting for transfers between devices: 52.3 us -> 59.3 us
  starting transfers between devices: 33.2 us -> 36.1 us
    ppermute x11, waiting for transfers between devices: 21.4 us -> 26.5 us  [cross(): return lax.ppermute(value, 'expert', [(i, i ^ 1) for i in range(devices)])]
    ppermute x10, waiting for transfers between devices: 29.1 us -> 32.4 us  [ring(): return lax.ppermute(value, 'expert', pairs)]
    ppermute x10, starting transfers between devices: 15.9 us -> 18.9 us  [ring(): return lax.ppermute(value, 'expert', pairs)]
    unnamed x47 -> x49, local copies, waits for them, and re-layouts: 8.09 us -> 9.66 us
  transfers between devices with their start and end apart: 30 -> 30, of which waited for: 16 -> 14; matrix products, arithmetic and copies ran while one was open for 42% -> 39% of each run, Pallas kernels for 0% -> 0%
where the time goes in v2:
time: 172 us
  waiting for transfers between devices  59.3 us (34%)
  matrix products  42.7 us (25%)
  starting transfers between devices  36.1 us (21%)
  local copies, waits for them, and re-layouts  16.3 us (9%)
  other arithmetic  15.8 us (9%)
    dot_general x24, matrix products, dot(): lax.dot_general(a, b, (((ca,), (cb,)), ((), ())), preferred_element_type=...  42.7 us
    ppermute x10, waiting for transfers between devices, ring(): return lax.ppermute(value, 'expert', pairs)  32.4 us
    ppermute x11, waiting for transfers between devices, cross(): return lax.ppermute(value, 'expert', [(i, i ^ 1) for i in range(devices)])  26.5 us
    ppermute x10, starting transfers between devices, ring(): return lax.ppermute(value, 'expert', pairs)  18.9 us
    ppermute x11, starting transfers between devices, cross(): return lax.ppermute(value, 'expert', [(i, i ^ 1) for i in range(devices)])  11.6 us
    unnamed x49, local copies, waits for them, and re-layouts  9.66 us
    ppermute x9, starting transfers between devices, swap(): return lax.ppermute(value, 'dp', [(i, i ^ bit) for i in range(groups)])  5.58 us
    squeeze x1, local copies, waits for them, and re-layouts, shards(): up_weight[e]  3.46 us
  transfers between devices with their start and end apart: 30, of which 14 were waited for; matrix products, arithmetic and copies ran while one was open for 39% of the time, Pallas kernels for 0%

profile of v2, /device:TPU:0, one launch (start us, length us, event | category | flops | bytes accessed | tf_op | source)
XLA Modules:
  0.0 171.8 jit_solution(469231687741034815)
XLA Ops:
  0.6 3.0 %collective-permute-start.1 = (bf16[128,2048]{1,0:T(8,128)(2,1)}, bf16[128,2048]{1,0:T(8,128)(2,1)}, u32[]{:S(2)}, u32[]{:S(2)}) collective-permute-start(bf16[128,2048]{1,0:T(8,128)(2,1)} %param.7), channel_id=1, source_target_pairs={{0,4},{4,0},{8,12},{12,8},{16,20},{20,16},{24,28},{28,24},{1,5},{5... | collective-permute-start | bytes 1572872 | tf_op jit(solution)/shard_map/ppermute | solution.py:35
  3.7 1.6 collective-permute-start
  7.2 1.9 %pad_maximum_fusion.17 = bf16[128,2176]{1,0:T(8,128)(2,1)} fusion(bf16[128,128]{1,0:T(8,128)(2,1)S(1)} %select_reduce_fusion, bf16[128,2048]{1,0:T(8,128)(2,1)} %param.8), kind=kLoop, calls=%fused_computation.114 | loop fusion | flops 1114112 | bytes 1114112 | tf_op jit(solution)/shard_map/concatenate | solution.py:47
  9.6 1.6 collective-permute-start.4
  11.2 3.5 %slice_bitcast_fusion.1 = (bf16[2048,384]{1,0:T(8,128)(2,1)S(1)}, bf16[2048,384]{1,0:T(8,128)(2,1)S(1)}, bf16[2048,384]{1,0:T(8,128)(2,1)S(1)}, bf16[2048,384]{1,0:T(8,128)(2,1)S(1)}) fusion(bf16[2,2048,384]{2,1,0:T(8,128)(2,1)} %param.12, bf16[2,2048,384]{2,1,0:T(8,128)(2,1)} %param.11), kind=kLoop, calls=%fused_computation.43 | loop fusion | bytes 12582912 | tf_op jit(solution)/shard_map/squeeze | solution.py:50
  14.6 3.1 %pad_maximum_fusion = bf16[2048,1536]{1,0:T(8,128)(2,1)} fusion(bf16[2048,384]{1,0:T(8,128)(2,1)S(1)} %get-tuple-element.199, bf16[2048,384]{1,0:T(8,128)(2,1)S(1)} %get-tuple-element.198, bf16[2048,384]{1,0:T(8,128)(2,1)S(1)} %get-tuple-element.260, bf16[2048,384]{1,0:T(8,128)(2,1)S(1)} %get-tuple-element.261), kind=kLoop, calls=%fused_computation | loop fusion | flops 25165824 | bytes 12582912 | tf_op jit(solution)/shard_map/concatenate | solution.py:49
  17.8 1.1 dynamic-slice_dynamic-update-slice_fusion.4
  19.0 1.1 constant_dynamic-update-slice_fusion.4
  20.6 1.1 collective-permute-start.3
  21.7 1.6 collective-permute-start.2
  23.3 1.1 dynamic-slice_dynamic-update-slice_fusion.3
  24.4 1.1 dynamic-slice_dynamic-update-slice_fusion.2
  25.5 5.0 %fusion.5 = f32[384,1536]{1,0:T(8,128)S(1)} fusion(bf16[2048,1536]{1,0:T(8,128)(2,1)} %pad_maximum_fusion, bf16[128,2048]{1,0:T(8,128)(2,1)} %collective-permute-done.1, bf16[128,2048]{1,0:T(8,128)(2,1)} %collective-permute-done, bf16[128,2048]{1,0:T(8,128)(2,1)S(1)} %copy-done.5), kind=kOutput, calls=%fused_computation.21 | convolution fusion | flops 2420637696 | bytes 10223616 | tf_op jit(solution)/shard_map/dot_general | solution.py:12
  30.6 2.0 %collective-permute-done.4 = bf16[128,2176]{1,0:T(8,128)(2,1)} collective-permute-done((bf16[128,2176]{1,0:T(8,128)(2,1)}, bf16[128,2176]{1,0:T(8,128)(2,1)}, u32[]{:S(2)}, u32[]{:S(2)}) %collective-permute-start.4) | collective-permute-done | bytes 557088 | tf_op jit(solution)/shard_map/ppermute | solution.py:32
  32.5 0.8 convert_reduce_fusion.6
  33.7 1.1 slice_dynamic-update-slice_fusion.3
  34.9 0.8 convert_reduce_fusion.5
  35.7 1.1 slice_dynamic-update-slice_fusion.2
  36.8 0.9 fusion.64
  38.0 3.3 %multiply_convert_fusion.1 = (bf16[384,768]{1,0:T(8,128)(2,1)S(1)}, bf16[384,768]{1,0:T(8,128)(2,1)S(1)}, bf16[384,768]{1,0:T(8,128)(2,1)S(1)}) fusion(f32[384,1536]{1,0:T(8,128)S(1)} %fusion.5, f32[384,384]{1,0:T(8,128)S(1)} %broadcast_in_dim.117, f32[384,384]{1,0:T(8,128)S(1)} %broadcast_in_dim.115, bf16[768,2048]{1,0:T(8,128)(2,1)S(1)} %bitcast.64, ...), kind=kOutput, calls=%fused_computation.57 | convolution fusion | flops 1219559424 | bytes 10125312 | tf_op jit(solution)/shard_map/dot_general | solution.py:12
  41.3 2.6 %convolution_convert_fusion.5 = bf16[384,2048]{1,0:T(8,128)(2,1)S(1)} fusion(bf16[2048,1536]{1,0:T(8,128)(2,1)S(1)} %bitcast.69, bf16[384,768]{1,0:T(8,128)(2,1)S(1)} %get-tuple-element.191, bf16[384,768]{1,0:T(8,128)(2,1)S(1)} %get-tuple-element.190), kind=kOutput, calls=%fused_computation.12 | convolution fusion | flops 2419064832 | bytes 9043968 | tf_op jit(solution)/shard_map/dot_general | solution.py:12
  44.2 1.8 %collective-permute-start.7 = (bf16[128,2048]{1,0:T(8,128)(2,1)S(1)}, bf16[128,2048]{1,0:T(8,128)(2,1)S(1)}, u32[]{:S(2)}, u32[]{:S(2)}) collective-permute-start(bf16[128,2048]{1,0:T(8,128)(2,1)S(1)} %collective-permute-done.2), channel_id=1, source_target_pairs={{0,4},{4,0},{8,12},{12,8},{16,20},{20,16},{24,28},{28,24},{1,5},{5... | collective-permute-start | bytes 1572872 | tf_op jit(solution)/shard_map/ppermute | solution.py:35
  46.0 1.3 collective-permute-start.6
  47.5 1.8 %fusion.28 = f32[256,1536]{1,0:T(8,128)S(1)} fusion(bf16[2048,1536]{1,0:T(8,128)(2,1)S(1)} %bitcast.69, bf16[128,2048]{1,0:T(8,128)(2,1)S(1)} %collective-permute-done.3, bf16[128,2048]{1,0:T(8,128)(2,1)S(1)} %collective-permute-done.2), kind=kOutput, calls=%fused_computation.62 | convolution fusion | flops 1612709888 | bytes 8912896 | tf_op jit(solution)/shard_map/dot_general | solution.py:12
  49.3 2.4 %collective-permute-done.9 = bf16[128,2176]{1,0:T(8,128)(2,1)S(1)} collective-permute-done((bf16[128,2176]{1,0:T(8,128)(2,1)}, bf16[128,2176]{1,0:T(8,128)(2,1)S(1)}, u32[]{:S(2)}, u32[]{:S(2)}) %collective-permute-start.9) | collective-permute-done | bytes 557088 | tf_op jit(solution)/shard_map/ppermute | solution.py:35
  51.7 3.9 %collective-permute-done.8 = bf16[128,2176]{1,0:T(8,128)(2,1)S(1)} collective-permute-done((bf16[128,2176]{1,0:T(8,128)(2,1)}, bf16[128,2176]{1,0:T(8,128)(2,1)S(1)}, u32[]{:S(2)}, u32[]{:S(2)}) %collective-permute-start.8) | collective-permute-done | bytes 557088 | tf_op jit(solution)/shard_map/ppermute | solution.py:32
  56.6 1.4 multiply_convert_fusion.9
  58.0 1.8 %convolution_convert_fusion.7 = bf16[256,2048]{1,0:T(8,128)(2,1)S(1)} fusion(bf16[2048,1536]{1,0:T(8,128)(2,1)S(1)} %bitcast.69, bf16[256,768]{1,0:T(8,128)(2,1)S(1)} %get-tuple-element.203, bf16[256,768]{1,0:T(8,128)(2,1)S(1)} %get-tuple-element.202), kind=kOutput, calls=%fused_computation.14 | convolution fusion | flops 1612709888 | bytes 8126464 | tf_op jit(solution)/shard_map/dot_general | solution.py:12
  60.0 3.0 %collective-permute-done.7 = bf16[128,2048]{1,0:T(8,128)(2,1)S(1)} collective-permute-done((bf16[128,2048]{1,0:T(8,128)(2,1)S(1)}, bf16[128,2048]{1,0:T(8,128)(2,1)S(1)}, u32[]{:S(2)}, u32[]{:S(2)}) %collective-permute-start.7) | collective-permute-done | bytes 524320 | tf_op jit(solution)/shard_map/ppermute | solution.py:35
  63.0 3.9 %collective-permute-done.6 = bf16[128,2048]{1,0:T(8,128)(2,1)S(1)} collective-permute-done((bf16[128,2048]{1,0:T(8,128)(2,1)S(1)}, bf16[128,2048]{1,0:T(8,128)(2,1)S(1)}, u32[]{:S(2)}, u32[]{:S(2)}) %collective-permute-start.6) | collective-permute-done | bytes 524320 | tf_op jit(solution)/shard_map/ppermute | solution.py:32
  67.3 2.1 %collective-permute-start.10 = (bf16[128,2176]{1,0:T(8,128)(2,1)}, bf16[128,2176]{1,0:T(8,128)(2,1)S(1)}, u32[]{:S(2)}, u32[]{:S(2)}) collective-permute-start(bf16[128,2176]{1,0:T(8,128)(2,1)} %collective-permute-done.5), channel_id=1, source_target_pairs={{0,24},{4,28},{8,0},{12,4},{16,8},{20,12},{24,16},{28,20},{1,25},{... | collective-permute-start | bytes 1671176 | tf_op jit(solution)/shard_map/ppermute | solution.py:32
  69.4 1.4 convolution_convert_fusion.2
  70.9 1.4 convolution_convert_fusion.3
  72.3 2.6 %convolution_convert_fusion.4 = bf16[512,1536]{1,0:T(8,128)(2,1)} fusion(bf16[640,512]{1,0:T(8,128)(2,1)S(1)} %get-tuple-element.243, bf16[640,1536]{1,0:T(8,128)(2,1)S(1)} %constant_dynamic-update-slice_fusion.5), kind=kOutput, calls=%fused_computation.11 | convolution fusion | flops 1007419392 | bytes 4194304 | tf_op jit(solution)/shard_map/dot_general | solution.py:12
  74.9 4.0 %convolution_convert_fusion = bf16[768,2048]{1,0:T(8,128)(2,1)} fusion(bf16[640,2048]{1,0:T(8,128)(2,1)S(1)} %slice_dynamic-update-slice_fusion, bf16[256,768]{1,0:T(8,128)(2,1)S(1)} %get-tuple-element.117, bf16[384,768]{1,0:T(8,128)(2,1)S(1)} %get-tuple-element.116), kind=kOutput, calls=%fused_computation.2 | convolution fusion | flops 2016804864 | bytes 6750208 | tf_op jit(solution)/shard_map/dot_general | solution.py:12
  78.9 1.4 convolution_convert_fusion.1
  80.3 1.8 %fusion.32 = f32[256,1536]{1,0:T(8,128)S(1)} fusion(bf16[2048,1536]{1,0:T(8,128)(2,1)S(1)} %bitcast.69, bf16[128,2048]{1,0:T(8,128)(2,1)S(1)} %collective-permute-done.7, bf16[128,2048]{1,0:T(8,128)(2,1)S(1)} %collective-permute-done.6), kind=kOutput, calls=%fused_computation.66 | convolution fusion | flops 1612709888 | bytes 8912896 | tf_op jit(solution)/shard_map/dot_general | solution.py:12
  82.7 1.4 multiply_convert_fusion.7
  84.1 1.8 %convolution_convert_fusion.6 = bf16[256,2048]{1,0:T(8,128)(2,1)S(1)} fusion(bf16[2048,1536]{1,0:T(8,128)(2,1)S(1)} %bitcast.69, bf16[256,768]{1,0:T(8,128)(2,1)S(1)} %get-tuple-element.201, bf16[256,768]{1,0:T(8,128)(2,1)S(1)} %get-tuple-element.200), kind=kOutput, calls=%fused_computation.13 | convolution fusion | flops 1612709888 | bytes 8126464 | tf_op jit(solution)/shard_map/dot_general | solution.py:12
  86.3 1.1 fusion.84
  87.3 2.1 %collective-permute-done.10 = bf16[128,2176]{1,0:T(8,128)(2,1)S(1)} collective-permute-done((bf16[128,2176]{1,0:T(8,128)(2,1)}, bf16[128,2176]{1,0:T(8,128)(2,1)S(1)}, u32[]{:S(2)}, u32[]{:S(2)}) %collective-permute-start.10) | collective-permute-done | bytes 557088 | tf_op jit(solution)/shard_map/ppermute | solution.py:32
  89.8 1.3 multiply_convert_fusion.11
  91.2 1.3 copy-done.6
  94.9 1.9 %add_convert_fusion = bf16[768,2048]{1,0:T(8,128)(2,1)S(1)} fusion(bf16[768,2048]{1,0:T(8,128)(2,1)S(1)} %copy-done.7, bf16[128,2048]{1,0:T(8,128)(2,1)S(1)} %slice-done.4, bf16[128,2048]{1,0:T(8,128)(2,1)S(1)} %slice-done.2, bf16[128,2048]{1,0:T(8,128)(2,1)S(1)} %slice-done.3, bf16[128,768]{1,0:T(8,128)(2,1)S(1)} %get-tuple-element.227, ...), kind=kOutput, calls=%fused_computation.1 | convolution fusion | flops 1218576384 | bytes 8454144 | tf_op jit(solution)/shard_map/dot_general | solution.py:12
  100.3 1.0 fusion.1
  102.0 1.5 collective-permute-start.22
  103.5 1.5 collective-permute-start.29
  105.0 11.2 %collective-permute-done.20 = bf16[128,2048]{1,0:T(8,128)(2,1)S(1)} collective-permute-done((bf16[128,2048]{1,0:T(8,128)(2,1)S(1)}, bf16[128,2048]{1,0:T(8,128)(2,1)S(1)}, u32[]{:S(2)}, u32[]{:S(2)}) %collective-permute-start.20) | collective-permute-done | bytes 524320 | tf_op jit(solution)/shard_map/ppermute | solution.py:35
  116.4 6.8 %collective-permute-start.21 = (bf16[128,2048]{1,0:T(8,128)(2,1)S(1)}, bf16[128,2048]{1,0:T(8,128)(2,1)S(1)}, u32[]{:S(2)}, u32[]{:S(2)}) collective-permute-start(bf16[128,2048]{1,0:T(8,128)(2,1)S(1)} %add_convert_fusion.10), channel_id=1, source_target_pairs={{0,24},{4,28},{8,0},{12,4},{16,8},{20,12},{24,16},{28,20},{1,25},{... | collective-permute-start | bytes 1572872 | tf_op jit(solution)/shard_map/ppermute | solution.py:32
  123.2 2.2 %convolution_convert_fusion.8 = bf16[128,2048]{1,0:T(8,128)(2,1)S(1)} fusion(bf16[128,1536]{1,0:T(8,128)(2,1)S(1)} %pad_maximum_fusion.25, bf16[2048,1536]{1,0:T(8,128)(2,1)S(1)} %bitcast.69), kind=kOutput, calls=%fused_computation.15 | convolution fusion | flops 805568512 | bytes 7208960 | tf_op jit(solution)/shard_map/dot_general | solution.py:12
  125.4 1.6 collective-permute-start.17
  127.5 1.2 fusion.2
  129.1 1.6 collective-permute-start.28
  130.7 4.4 %collective-permute-done.21 = bf16[128,2048]{1,0:T(8,128)(2,1)S(1)} collective-permute-done((bf16[128,2048]{1,0:T(8,128)(2,1)S(1)}, bf16[128,2048]{1,0:T(8,128)(2,1)S(1)}, u32[]{:S(2)}, u32[]{:S(2)}) %collective-permute-start.21) | collective-permute-done | bytes 524320 | tf_op jit(solution)/shard_map/ppermute | solution.py:32
  135.1 6.7 %collective-permute-done.26 = bf16[128,2048]{1,0:T(8,128)(2,1)S(1)} collective-permute-done((bf16[128,2048]{1,0:T(8,128)(2,1)S(1)}, bf16[128,2048]{1,0:T(8,128)(2,1)S(1)}, u32[]{:S(2)}, u32[]{:S(2)}) %collective-permute-start.26) | collective-permute-done | bytes 524320 | tf_op jit(solution)/shard_map/ppermute | solution.py:35
  142.2 3.9 %collective-permute-start.25 = (bf16[128,2048]{1,0:T(8,128)(2,1)S(1)}, bf16[128,2048]{1,0:T(8,128)(2,1)S(1)}, u32[]{:S(2)}, u32[]{:S(2)}) collective-permute-start(bf16[128,2048]{1,0:T(8,128)(2,1)S(1)} %add_convert_fusion.9), channel_id=1, source_target_pairs={{0,24},{4,28},{8,0},{12,4},{16,8},{20,12},{24,16},{28,20},{1,25},{... | collective-permute-start | bytes 1572872 | tf_op jit(solution)/shard_map/ppermute | solution.py:32
  146.1 1.4 collective-permute-start.19
  147.8 1.0 pad_maximum_fusion.15
  148.8 3.2 %collective-permute-done.28 = bf16[128,2048]{1,0:T(8,128)(2,1)S(1)} collective-permute-done((bf16[128,2048]{1,0:T(8,128)(2,1)S(1)}, bf16[128,2048]{1,0:T(8,128)(2,1)S(1)}, u32[]{:S(2)}, u32[]{:S(2)}) %collective-permute-start.28) | collective-permute-done | bytes 524320 | tf_op jit(solution)/shard_map/ppermute | solution.py:35
  152.0 6.7 %collective-permute-done.27 = bf16[128,2048]{1,0:T(8,128)(2,1)S(1)} collective-permute-done((bf16[128,2048]{1,0:T(8,128)(2,1)S(1)}, bf16[128,2048]{1,0:T(8,128)(2,1)S(1)}, u32[]{:S(2)}, u32[]{:S(2)}) %collective-permute-start.27) | collective-permute-done | bytes 524320 | tf_op jit(solution)/shard_map/ppermute | solution.py:32
  158.7 8.9 %collective-permute-done.25 = bf16[128,2048]{1,0:T(8,128)(2,1)S(1)} collective-permute-done((bf16[128,2048]{1,0:T(8,128)(2,1)S(1)}, bf16[128,2048]{1,0:T(8,128)(2,1)S(1)}, u32[]{:S(2)}, u32[]{:S(2)}) %collective-permute-start.25) | collective-permute-done | bytes 524320 | tf_op jit(solution)/shard_map/ppermute | solution.py:32
  167.6 1.1 add_convert_fusion.7
  169.7 1.0 pad_maximum_fusion.16
  170.7 1.2 fusion.20
  (142 shorter events, 16.0 us)
Async XLA Ops:
  0.6 37.0 %copy-start = (bf16[2,384,2048]{2,1,0:T(8,128)(2,1)S(1)}, bf16[2,384,2048]{2,1,0:T(8,128)(2,1)}, u32[]{:S(2)}) copy-start(bf16[2,384,2048]{2,1,0:T(8,128)(2,1)} %param.13) | copy-start | bytes 9437188
  0.6 19.5 %collective-permute-start.1 = (bf16[128,2048]{1,0:T(8,128)(2,1)}, bf16[128,2048]{1,0:T(8,128)(2,1)}, u32[]{:S(2)}, u32[]{:S(2)}) collective-permute-start(bf16[128,2048]{1,0:T(8,128)(2,1)} %param.7), channel_id=1, source_target_pairs={{0,4},{4,0},{8,12},{12,8},{16,20},{20,16},{24,28},{28,24},{1,5},{5... | collective-permute-start | bytes 1572872 | tf_op jit(solution)/shard_map/ppermute | solution.py:35
  3.7 17.0 %collective-permute-start = (bf16[128,2048]{1,0:T(8,128)(2,1)}, bf16[128,2048]{1,0:T(8,128)(2,1)}, u32[]{:S(2)}, u32[]{:S(2)}) collective-permute-start(bf16[128,2048]{1,0:T(8,128)(2,1)} %param.7), channel_id=1, source_target_pairs={{0,8},{4,12},{8,16},{12,20},{16,24},{20,28},{24,0},{28,4},{1,9},{5... | collective-permute-start | bytes 1572872 | tf_op jit(solution)/shard_map/ppermute | solution.py:32
  9.1 21.5 %collective-permute-start.5 = (bf16[128,2176]{1,0:T(8,128)(2,1)}, bf16[128,2176]{1,0:T(8,128)(2,1)}, u32[]{:S(2)}, u32[]{:S(2)}) collective-permute-start(bf16[128,2176]{1,0:T(8,128)(2,1)} %pad_maximum_fusion.17), channel_id=1, source_target_pairs={{0,4},{4,0},{8,12},{12,8},{16,20},{20,16},{24,28},{28,24},{1,5},{5... | collective-permute-start | bytes 1671176 | tf_op jit(solution)/shard_map/ppermute | solution.py:35
  9.6 23.0 %collective-permute-start.4 = (bf16[128,2176]{1,0:T(8,128)(2,1)}, bf16[128,2176]{1,0:T(8,128)(2,1)}, u32[]{:S(2)}, u32[]{:S(2)}) collective-permute-start(bf16[128,2176]{1,0:T(8,128)(2,1)} %pad_maximum_fusion.17), channel_id=1, source_target_pairs={{0,8},{4,12},{8,16},{12,20},{16,24},{20,28},{24,0},{28,4},{1,9},{5... | collective-permute-start | bytes 1671176 | tf_op jit(solution)/shard_map/ppermute | solution.py:32
  18.9 6.6 %copy-start.5 = (bf16[128,2048]{1,0:T(8,128)(2,1)S(1)}, bf16[128,2048]{1,0:T(8,128)(2,1)}, u32[]{:S(2)}) copy-start(bf16[128,2048]{1,0:T(8,128)(2,1)} %param.7) | copy-start | bytes 1572868
  20.6 23.6 %collective-permute-start.3 = (bf16[128,2048]{1,0:T(8,128)(2,1)}, bf16[128,2048]{1,0:T(8,128)(2,1)S(1)}, u32[]{:S(2)}, u32[]{:S(2)}) collective-permute-start(bf16[128,2048]{1,0:T(8,128)(2,1)} %collective-permute-done), channel_id=1, source_target_pairs={{0,4},{4,0},{8,12},{12,8},{16,20},{20,16},{24,28},{28,24},{1,5},{5... | collective-permute-start | bytes 1572872 | tf_op jit(solution)/shard_map/ppermute | solution.py:35
  21.7 22.5 %collective-permute-start.2 = (bf16[128,2048]{1,0:T(8,128)(2,1)}, bf16[128,2048]{1,0:T(8,128)(2,1)S(1)}, u32[]{:S(2)}, u32[]{:S(2)}) collective-permute-start(bf16[128,2048]{1,0:T(8,128)(2,1)} %collective-permute-done), channel_id=1, source_target_pairs={{0,8},{4,12},{8,16},{12,20},{16,24},{20,28},{24,0},{28,4},{1,9},{5... | collective-permute-start | bytes 1572872 | tf_op jit(solution)/shard_map/ppermute | solution.py:32
  30.5 6.2 %copy-start.1 = (bf16[128,2048]{1,0:T(8,128)(2,1)S(1)}, bf16[128,2048]{1,0:T(8,128)(2,1)}, u32[]{:S(2)}) copy-start(bf16[128,2048]{1,0:T(8,128)(2,1)} %param.8) | copy-start | bytes 1572868
  33.3 18.4 %collective-permute-start.9 = (bf16[128,2176]{1,0:T(8,128)(2,1)}, bf16[128,2176]{1,0:T(8,128)(2,1)S(1)}, u32[]{:S(2)}, u32[]{:S(2)}) collective-permute-start(bf16[128,2176]{1,0:T(8,128)(2,1)} %collective-permute-done.4), channel_id=1, source_target_pairs={{0,4},{4,0},{8,12},{12,8},{16,20},{20,16},{24,28},{28,24},{1,5},{5... | collective-permute-start | bytes 1671176 | tf_op jit(solution)/shard_map/ppermute | solution.py:35
  33.7 21.9 %collective-permute-start.8 = (bf16[128,2176]{1,0:T(8,128)(2,1)}, bf16[128,2176]{1,0:T(8,128)(2,1)S(1)}, u32[]{:S(2)}, u32[]{:S(2)}) collective-permute-start(bf16[128,2176]{1,0:T(8,128)(2,1)} %collective-permute-done.4), channel_id=1, source_target_pairs={{0,8},{4,12},{8,16},{12,20},{16,24},{20,28},{24,0},{28,4},{1,9},{5... | collective-permute-start | bytes 1671176 | tf_op jit(solution)/shard_map/ppermute | solution.py:32
  37.8 3.4 %slice-start = ((s8[6291456]{0:T(1024)(128)(4,1)}), s8[4194304]{0:T(1024)(128)(4,1)S(1)}, s32[]{:S(2)}) async-start(s8[6291456]{0:T(1024)(128)(4,1)} %bitcast.68), calls=%async_computation | async-start | bytes 8388608
  37.9 3.3 %slice-start.1 = ((s8[6291456]{0:T(1024)(128)(4,1)}), s8[2097152]{0:T(1024)(128)(4,1)S(1)}, s32[]{:S(2)}) async-start(s8[6291456]{0:T(1024)(128)(4,1)} %bitcast.68), calls=%async_computation.1 | async-start | bytes 4194304
  44.2 18.8 %collective-permute-start.7 = (bf16[128,2048]{1,0:T(8,128)(2,1)S(1)}, bf16[128,2048]{1,0:T(8,128)(2,1)S(1)}, u32[]{:S(2)}, u32[]{:S(2)}) collective-permute-start(bf16[128,2048]{1,0:T(8,128)(2,1)S(1)} %collective-permute-done.2), channel_id=1, source_target_pairs={{0,4},{4,0},{8,12},{12,8},{16,20},{20,16},{24,28},{28,24},{1,5},{5... | collective-permute-start | bytes 1572872 | tf_op jit(solution)/shard_map/ppermute | solution.py:35
  46.0 20.9 %collective-permute-start.6 = (bf16[128,2048]{1,0:T(8,128)(2,1)S(1)}, bf16[128,2048]{1,0:T(8,128)(2,1)S(1)}, u32[]{:S(2)}, u32[]{:S(2)}) collective-permute-start(bf16[128,2048]{1,0:T(8,128)(2,1)S(1)} %collective-permute-done.2), channel_id=1, source_target_pairs={{0,8},{4,12},{8,16},{12,20},{16,24},{20,28},{24,0},{28,4},{1,9},{5... | collective-permute-start | bytes 1572872 | tf_op jit(solution)/shard_map/ppermute | solution.py:32
  55.6 26.5 %collective-permute-start.13 = (bf16[128,2176]{1,0:T(8,128)(2,1)S(1)}, bf16[128,2176]{1,0:T(8,128)(2,1)S(1)}, u32[]{:S(2)}, u32[]{:S(2)}) collective-permute-start(bf16[128,2176]{1,0:T(8,128)(2,1)S(1)} %collective-permute-done.8), channel_id=1, source_target_pairs={{0,4},{4,0},{8,12},{12,8},{16,20},{20,16},{24,28},{28,24},{1,5},{5... | collective-permute-start | bytes 1671176 | tf_op jit(solution)/shard_map/ppermute | solution.py:35
  56.0 26.1 %collective-permute-start.12 = (bf16[128,2176]{1,0:T(8,128)(2,1)S(1)}, bf16[128,2176]{1,0:T(8,128)(2,1)S(1)}, u32[]{:S(2)}, u32[]{:S(2)}) collective-permute-start(bf16[128,2176]{1,0:T(8,128)(2,1)S(1)} %collective-permute-done.8), channel_id=1, source_target_pairs={{0,8},{4,12},{8,16},{12,20},{16,24},{20,28},{24,0},{28,4},{1,9},{5... | collective-permute-start | bytes 1671176 | tf_op jit(solution)/shard_map/ppermute | solution.py:32
  66.9 19.2 %collective-permute-start.11 = (bf16[128,2048]{1,0:T(8,128)(2,1)S(1)}, bf16[128,2048]{1,0:T(8,128)(2,1)S(1)}, u32[]{:S(2)}, u32[]{:S(2)}) collective-permute-start(bf16[128,2048]{1,0:T(8,128)(2,1)S(1)} %collective-permute-done.6), channel_id=1, source_target_pairs={{0,4},{4,0},{8,12},{12,8},{16,20},{20,16},{24,28},{28,24},{1,5},{5... | collective-permute-start | bytes 1572872 | tf_op jit(solution)/shard_map/ppermute | solution.py:35
  67.3 22.1 %collective-permute-start.10 = (bf16[128,2176]{1,0:T(8,128)(2,1)}, bf16[128,2176]{1,0:T(8,128)(2,1)S(1)}, u32[]{:S(2)}, u32[]{:S(2)}) collective-permute-start(bf16[128,2176]{1,0:T(8,128)(2,1)} %collective-permute-done.5), channel_id=1, source_target_pairs={{0,24},{4,28},{8,0},{12,4},{16,8},{20,12},{24,16},{28,20},{1,25},{... | collective-permute-start | bytes 1671176 | tf_op jit(solution)/shard_map/ppermute | solution.py:32
  82.1 3.8 %copy-start.2 = (bf16[128,2176]{1,0:T(8,128)(2,1)}, bf16[128,2176]{1,0:T(8,128)(2,1)S(1)}, u32[]{:S(2)}) copy-start(bf16[128,2176]{1,0:T(8,128)(2,1)S(1)} %collective-permute-done.13) | copy-start | bytes 1671172
  82.2 3.8 %copy-start.3 = (bf16[128,2176]{1,0:T(8,128)(2,1)}, bf16[128,2176]{1,0:T(8,128)(2,1)S(1)}, u32[]{:S(2)}) copy-start(bf16[128,2176]{1,0:T(8,128)(2,1)S(1)} %collective-permute-done.12) | copy-start | bytes 1671172
  89.5 1.6 copy-start.4
  91.1 1.4 copy-start.6
  92.5 2.0 %copy-start.7 = (bf16[768,2048]{1,0:T(8,128)(2,1)S(1)}, bf16[768,2048]{1,0:T(8,128)(2,1)}, u32[]{:S(2)}) copy-start(bf16[768,2048]{1,0:T(8,128)(2,1)} %convolution_convert_fusion) | copy-start | bytes 9437188
  93.1 1.5 slice-start.2
  93.1 1.7 slice-start.3
  93.1 1.8 %slice-start.4 = ((bf16[128,2176]{1,0:T(8,128)(2,1)}), bf16[128,2048]{1,0:T(8,128)(2,1)S(1)}, s32[]{:S(2)}) async-start(bf16[128,2176]{1,0:T(8,128)(2,1)} %copy-done.4), calls=%async_computation.4 | async-start | bytes 1048576 | tf_op jit(solution)/shard_map/slice | solution.py:56
  93.1 3.7 %collective-permute-start.15 = (bf16[512,768]{1,0:T(8,128)(2,1)S(1)}, bf16[512,768]{1,0:T(8,128)(2,1)S(1)}, u32[]{:S(2)}, u32[]{:S(2)}) collective-permute-start(bf16[512,768]{1,0:T(8,128)(2,1)S(1)} %add_convert_fusion.6), channel_id=1, source_target_pairs={{0,1},{1,0},{2,3},{3,2},{4,5},{5,4},{6,7},{7,6},{8,9},{9,8},{10,11... | collective-permute-start | bytes 2359304 | tf_op jit(solution)/shard_map/ppermute | solution.py:38
  93.2 7.0 %collective-permute-start.18 = (f32[1,128]{1,0:T(1,128)S(1)}, f32[1,128]{1,0:T(1,128)S(1)}, u32[]{:S(2)}, u32[]{:S(2)}) collective-permute-start(f32[1,128]{1,0:T(1,128)S(1)} %add_bitcast_fusion), channel_id=1, source_target_pairs={{0,1},{1,0},{2,3},{3,2},{4,5},{5,4},{6,7},{7,6},{8,9},{9,8},{10,11... | collective-permute-start | bytes 1544 | tf_op jit(solution)/shard_map/ppermute | solution.py:38
  94.4 3.4 %collective-permute-start.14 = (bf16[512,768]{1,0:T(8,128)(2,1)S(1)}, bf16[512,768]{1,0:T(8,128)(2,1)S(1)}, u32[]{:S(2)}, u32[]{:S(2)}) collective-permute-start(bf16[512,768]{1,0:T(8,128)(2,1)S(1)} %add_convert_fusion.5), channel_id=1, source_target_pairs={{0,1},{1,0},{2,3},{3,2},{4,5},{5,4},{6,7},{7,6},{8,9},{9,8},{10,11... | collective-permute-start | bytes 2359304 | tf_op jit(solution)/shard_map/ppermute | solution.py:38
  97.1 2.4 %collective-permute-start.16 = (bf16[2,96,2048]{2,1,0:T(8,128)(2,1)S(1)}, bf16[2,96,2048]{2,1,0:T(8,128)(2,1)S(1)}, u32[]{:S(2)}, u32[]{:S(2)}) collective-permute-start(bf16[2,96,2048]{2,1,0:T(8,128)(2,1)S(1)} %get-tuple-element.195), channel_id=1, source_target_pairs={{0,1},{1,0},{2,3},{3,2},{4,5},{5,4},{6,7},{7,6},{8,9},{9,8},{10,11... | collective-permute-start | bytes 2359304 | tf_op jit(solution)/shard_map/ppermute | solution.py:38
  101.3 25.7 %collective-permute-start.23 = (bf16[512,1536]{1,0:T(8,128)(2,1)S(1)}, bf16[512,1536]{1,0:T(8,128)(2,1)S(1)}, u32[]{:S(2)}, u32[]{:S(2)}) collective-permute-start(bf16[512,1536]{1,0:T(8,128)(2,1)S(1)} %fusion.1), channel_id=1, source_target_pairs={{0,1},{1,0},{2,3},{3,2},{4,5},{5,4},{6,7},{7,6},{8,9},{9,8},{10,11... | collective-permute-start | bytes 4718600 | tf_op jit(solution)/shard_map/ppermute | solution.py:38
  101.5 14.8 %collective-permute-start.20 = (bf16[128,2048]{1,0:T(8,128)(2,1)S(1)}, bf16[128,2048]{1,0:T(8,128)(2,1)S(1)}, u32[]{:S(2)}, u32[]{:S(2)}) collective-permute-start(bf16[128,2048]{1,0:T(8,128)(2,1)S(1)} %get-tuple-element.145), channel_id=1, source_target_pairs={{0,4},{4,0},{8,12},{12,8},{16,20},{20,16},{24,28},{28,24},{1,5},{5... | collective-permute-start | bytes 1572872 | tf_op jit(solution)/shard_map/ppermute | solution.py:35
  102.0 27.1 %collective-permute-start.22 = (bf16[128,2048]{1,0:T(8,128)(2,1)S(1)}, bf16[128,2048]{1,0:T(8,128)(2,1)S(1)}, u32[]{:S(2)}, u32[]{:S(2)}) collective-permute-start(bf16[128,2048]{1,0:T(8,128)(2,1)S(1)} %get-tuple-element.147), channel_id=1, source_target_pairs={{0,4},{4,0},{8,12},{12,8},{16,20},{20,16},{24,28},{28,24},{1,5},{5... | collective-permute-start | bytes 1572872 | tf_op jit(solution)/shard_map/ppermute | solution.py:35
  103.5 42.6 %collective-permute-start.29 = (bf16[512,768]{1,0:T(8,128)(2,1)S(1)}, bf16[512,768]{1,0:T(8,128)(2,1)S(1)}, u32[]{:S(2)}, u32[]{:S(2)}) collective-permute-start(bf16[512,768]{1,0:T(8,128)(2,1)S(1)} %get-tuple-element.212), channel_id=1, source_target_pairs={{0,2},{1,3},{2,0},{3,1},{4,6},{5,7},{6,4},{7,5},{8,10},{9,11},{10,... | collective-permute-start | bytes 2359304 | tf_op jit(solution)/shard_map/ppermute | solution.py:38
  116.3 9.1 %collective-permute-start.24 = (bf16[2,96,2048]{2,1,0:T(8,128)(2,1)S(1)}, bf16[2,96,2048]{2,1,0:T(8,128)(2,1)S(1)}, u32[]{:S(2)}, u32[]{:S(2)}) collective-permute-start(bf16[2,96,2048]{2,1,0:T(8,128)(2,1)S(1)} %get-tuple-element.152), channel_id=1, source_target_pairs={{0,1},{1,0},{2,3},{3,2},{4,5},{5,4},{6,7},{7,6},{8,9},{9,8},{10,11... | collective-permute-start | bytes 2359304 | tf_op jit(solution)/shard_map/ppermute | solution.py:38
  116.4 18.7 %collective-permute-start.21 = (bf16[128,2048]{1,0:T(8,128)(2,1)S(1)}, bf16[128,2048]{1,0:T(8,128)(2,1)S(1)}, u32[]{:S(2)}, u32[]{:S(2)}) collective-permute-start(bf16[128,2048]{1,0:T(8,128)(2,1)S(1)} %add_convert_fusion.10), channel_id=1, source_target_pairs={{0,24},{4,28},{8,0},{12,4},{16,8},{20,12},{24,16},{28,20},{1,25},{... | collective-permute-start | bytes 1572872 | tf_op jit(solution)/shard_map/ppermute | solution.py:32
  125.4 43.3 %collective-permute-start.17 = (bf16[3072,256]{1,0:T(8,128)(2,1)S(1)}, bf16[3072,256]{1,0:T(8,128)(2,1)S(1)}, u32[]{:S(2)}, u32[]{:S(2)}) collective-permute-start(bf16[3072,256]{1,0:T(8,128)(2,1)S(1)} %constant_dynamic-update-slice_fusion.7), channel_id=1, source_target_pairs={{0,2},{1,3},{2,0},{3,1},{4,6},{5,7},{6,4},{7,5},{8,10},{9,11},{10,... | collective-permute-start | bytes 4718600 | tf_op jit(solution)/shard_map/ppermute | solution.py:38
  127.0 14.8 %collective-permute-start.26 = (bf16[128,2048]{1,0:T(8,128)(2,1)S(1)}, bf16[128,2048]{1,0:T(8,128)(2,1)S(1)}, u32[]{:S(2)}, u32[]{:S(2)}) collective-permute-start(bf16[128,2048]{1,0:T(8,128)(2,1)S(1)} %convolution_convert_fusion.8), channel_id=1, source_target_pairs={{0,4},{4,0},{8,12},{12,8},{16,20},{20,16},{24,28},{28,24},{1,5},{5... | collective-permute-start | bytes 1572872 | tf_op jit(solution)/shard_map/ppermute | solution.py:35
  129.1 22.9 %collective-permute-start.28 = (bf16[128,2048]{1,0:T(8,128)(2,1)S(1)}, bf16[128,2048]{1,0:T(8,128)(2,1)S(1)}, u32[]{:S(2)}, u32[]{:S(2)}) collective-permute-start(bf16[128,2048]{1,0:T(8,128)(2,1)S(1)} %get-tuple-element.168), channel_id=1, source_target_pairs={{0,4},{4,0},{8,12},{12,8},{16,20},{20,16},{24,28},{28,24},{1,5},{5... | collective-permute-start | bytes 1572872 | tf_op jit(solution)/shard_map/ppermute | solution.py:35
  141.9 16.8 %collective-permute-start.27 = (bf16[128,2048]{1,0:T(8,128)(2,1)S(1)}, bf16[128,2048]{1,0:T(8,128)(2,1)S(1)}, u32[]{:S(2)}, u32[]{:S(2)}) collective-permute-start(bf16[128,2048]{1,0:T(8,128)(2,1)S(1)} %add_convert_fusion.8), channel_id=1, source_target_pairs={{0,8},{4,12},{8,16},{12,20},{16,24},{20,28},{24,0},{28,4},{1,9},{5... | collective-permute-start | bytes 1572872 | tf_op jit(solution)/shard_map/ppermute | solution.py:32
  142.2 25.3 %collective-permute-start.25 = (bf16[128,2048]{1,0:T(8,128)(2,1)S(1)}, bf16[128,2048]{1,0:T(8,128)(2,1)S(1)}, u32[]{:S(2)}, u32[]{:S(2)}) collective-permute-start(bf16[128,2048]{1,0:T(8,128)(2,1)S(1)} %add_convert_fusion.9), channel_id=1, source_target_pairs={{0,24},{4,28},{8,0},{12,4},{16,8},{20,12},{24,16},{28,20},{1,25},{... | collective-permute-start | bytes 1572872 | tf_op jit(solution)/shard_map/ppermute | solution.py:32
  146.1 22.6 %collective-permute-start.19 = (f32[1,128]{1,0:T(1,128)S(1)}, f32[1,128]{1,0:T(1,128)S(1)}, u32[]{:S(2)}, u32[]{:S(2)}) collective-permute-start(f32[1,128]{1,0:T(1,128)S(1)} %add.275), channel_id=1, source_target_pairs={{0,2},{1,3},{2,0},{3,1},{4,6},{5,7},{6,4},{7,5},{8,10},{9,11},{10,... | collective-permute-start | bytes 1544 | tf_op jit(solution)/shard_map/ppermute | solution.py:38
